TPU v7x, 128 devices: a whole 4x4x4 slice. The times are simulated.
128 devices in a mesh: grp: 8 (over z, core), dev: 16 (over x, y).
Axes of the slice: x: 4, y: 4, z: 4, core: 2. Of those that a mesh axis runs over, the one named last changes fastest.
Arguments:
- start: float32 [32, 262144], P(None, ('grp', 'dev')), may hold values from -6 to 6
- near_blocks: bfloat16 [20480, 256, 256], P(('grp', 'dev')), may hold values from -0.375 to 0.375
- near_rows: int32 [20480], P(('grp', 'dev')), may hold values from 0 to 127, as said below
- near_cols: int32 [20480], P(('grp', 'dev')), may hold values from 0 to 143, as said below
- near_scale: int32 [20480], P(('grp', 'dev')), may hold values from 0 to 255
- scale_table: float32 [256], replicated, may hold values from 0.05 to 0.5
- near_live: int32 [128], P(('grp', 'dev')), may hold values from 40 to 160, as said below
- leaf_basis: bfloat16 [1024, 64, 256], P(('grp', 'dev')), may hold values from -0.375 to 0.375
- leaf_transfer: float32 [1024, 64, 64], P(('grp', 'dev')), may hold values from -0.25 to 0.25
- device_transfer: float32 [128, 64, 64], P(('grp', 'dev')), may hold values from -0.1875 to 0.1875
- device_coupling: float32 [30, 64, 64], replicated, may hold values from -0.125 to 0.125
- group_coupling: float32 [6, 64, 64], replicated, may hold values from -0.75 to 0.75
Outputs:
- next_basis: float32 [32, 262144], P(None, ('grp', 'dev'))
- hessenberg: float32 [5, 32, 32], replicated
Inputs may be any that keep to these rules, and one draw needn't show every extreme that they name: `near_rows`: within each group of 16 devices every cluster of the group is the row of some block slot whose column is the same cluster. `near_cols`: A block's column cluster lies between its row cluster and 16 clusters past it; in the last group it stays below 128. `near_live`: slots below this count are used; in every group one device uses all its slots.
All inputs are finite; a program needn't handle non-finite values.
Results may differ from a plain program's by a relative error of at most 0.0043.
Values may be sent and summed in bfloat16 or wider, within the bound.
A program may use at most 128 MiB of HBM per device.

v0:
```python
import jax
import jax.numpy as jnp
from jax import lax
from jax.sharding import PartitionSpec as P

P_SIZE = 256
REACH = 16


HIGHEST = lax.Precision.HIGHEST


def extended(cells, sides, width):
    for axis, dim in sides:
        count = lax.axis_size(axis)
        ends = count - 1
        head = lax.slice_in_dim(cells, 0, width, axis=dim)
        tail = lax.slice_in_dim(cells, cells.shape[dim] - width, cells.shape[dim], axis=dim)
        cells = jnp.concatenate(
            [
                lax.ppermute(tail, axis, [(i, (i + 1) % count) for i in range(ends)]),
                cells,
                lax.ppermute(head, axis, [((i + 1) % count, i) for i in range(ends)]),
            ],
            axis=dim,
        )
    return cells


def from_behind(value, axis, steps):
    count = lax.axis_size(axis)
    initial, last = (max(0, -steps), min(count, count - steps))
    return lax.ppermute(value, axis, [(source, source + steps) for source in range(initial, last)])


def select_coupling(offsets, table):
    index_range = jnp.arange(table.shape[0], dtype=jnp.int32)
    ahead = (offsets[:, None] - 2 == index_range[None, :]).astype(jnp.float32)
    behind = (-offsets[:, None] - 2 == index_range[None, :]).astype(jnp.float32)
    return jnp.einsum("wo,ojk->wjk", ahead, table, precision=HIGHEST) + jnp.einsum(
        "wo,okj->wjk", behind, table, precision=HIGHEST
    )


def near_window(window, near_blocks, near_rows, near_cols, weights):
    column_values = jnp.take(window, near_cols, axis=1)
    row_values = jnp.take(window, near_rows, axis=1)
    to_rows = (
        jnp.einsum("kij,rkj->rki", near_blocks, column_values, preferred_element_type=jnp.float32)
        * weights[None, :, None]
    )
    to_columns = (
        jnp.einsum("kij,rki->rkj", near_blocks, row_values, preferred_element_type=jnp.float32)
        * weights[None, :, None]
    )
    totals = jnp.zeros(window.shape, jnp.float32)
    return totals.at[:, near_rows].add(to_rows).at[:, near_cols].add(to_columns)


def far_field(
    own_values, leaf_basis, leaf_transfer, device_transfer, device_coupling, group_coupling
):
    device_count = lax.axis_size("dev")
    group_count = lax.axis_size("grp")
    device_place = lax.axis_index("dev")
    group_place = lax.axis_index("grp")
    cases = own_values.shape[0]
    clusters = leaf_basis.shape[0]
    panel_size = leaf_basis.shape[2]
    panels = own_values.reshape(cases, clusters, panel_size)
    leaf_coeffs = jnp.einsum("ckp,rcp->ckr", leaf_basis, panels, preferred_element_type=jnp.float32)
    own_coeffs = jnp.einsum("cjk,ckr->jr", leaf_transfer, leaf_coeffs, precision=HIGHEST)
    parent_part = jnp.dot(device_transfer[0], own_coeffs, precision=HIGHEST)
    group_coeffs, group_parents = (
        lax.all_gather(own_coeffs[None], "dev", axis=0, tiled=True),
        lax.all_gather(parent_part[None], "dev", axis=0, tiled=True),
    )
    beside_all = extended(group_coeffs, (("grp", 0),), device_count)
    top_coeffs = lax.all_gather(jnp.sum(group_parents, axis=0)[None], "grp", axis=0, tiled=True)
    offsets = jnp.arange(3 * device_count, dtype=jnp.int32) - (device_count + device_place)
    field = jnp.einsum(
        "wjk,wkr->jr", select_coupling(offsets, device_coupling), beside_all, precision=HIGHEST
    )
    top_offsets = jnp.arange(group_count, dtype=jnp.int32) - group_place
    top_field = jnp.einsum(
        "wjk,wkr->jr", select_coupling(top_offsets, group_coupling), top_coeffs, precision=HIGHEST
    )
    field = field + jnp.dot(device_transfer[0].T, top_field, precision=HIGHEST)
    leaf_fields = jnp.einsum("ckj,kr->cjr", leaf_transfer, field, precision=HIGHEST)
    basis_wide = leaf_basis.astype(jnp.float32)
    far_values = jnp.einsum("ckp,ckr->rcp", basis_wide, leaf_fields, precision=HIGHEST)
    return far_values.reshape(cases, clusters * panel_size)


def operator_parts(
    group_values,
    own_values,
    near_blocks,
    near_rows,
    near_cols,
    weights,
    leaf_basis,
    leaf_transfer,
    device_transfer,
    device_coupling,
    group_coupling,
):
    reach_width = REACH * P_SIZE
    cases = group_values.shape[0]
    following = from_behind(group_values[:, :reach_width], "grp", -1)
    window = jnp.concatenate([group_values, following], axis=1).reshape(cases, -1, P_SIZE)
    totals = near_window(window, near_blocks, near_rows, near_cols, weights)
    group_clusters = window.shape[1] - REACH
    overflow = from_behind(totals[:, group_clusters:], "grp", 1)
    leading = totals[:, :REACH] + overflow
    near_part = jnp.concatenate([leading, totals[:, REACH:group_clusters]], axis=1).reshape(
        cases, -1
    )
    far_part = far_field(
        own_values, leaf_basis, leaf_transfer, device_transfer, device_coupling, group_coupling
    )
    return (near_part, far_part)


def global_inner(stacked, total_panels):
    summed = lax.psum(stacked, ("grp", "dev"))
    return summed / total_panels


def orthonormal(panel_block, total_panels):
    gram = global_inner(jnp.dot(panel_block, panel_block.T, precision=HIGHEST)[None], total_panels)[
        0
    ]
    factor = jnp.linalg.cholesky(gram)
    return (lax.linalg.triangular_solve(factor, panel_block, left_side=True, lower=True), factor)


def next_block(product_block, bases, total_panels):
    inner_terms = [jnp.dot(basis_item, product_block.T, precision=HIGHEST) for basis_item in bases]
    summed = global_inner(jnp.stack(inner_terms), total_panels)
    projections = [summed[index] for index in range(len(bases))]
    remainder = product_block
    for projection, basis_item in zip(projections, bases):
        remainder = remainder - jnp.dot(projection.T, basis_item, precision=HIGHEST)
    new_basis, factor = orthonormal(remainder, total_panels)
    return (new_basis, projections, factor)


def shards(
    start,
    near_blocks,
    near_rows,
    near_cols,
    near_scale,
    scale_table,
    near_live,
    leaf_basis,
    leaf_transfer,
    device_transfer,
    device_coupling,
    group_coupling,
):
    device_count = lax.axis_size("dev")
    group_count = lax.axis_size("grp")
    own_width = start.shape[1]
    total_panels = own_width * device_count * group_count
    slot_count = near_scale.shape[0]
    scale_pick = (
        near_scale[:, None] == jnp.arange(scale_table.shape[0], dtype=jnp.int32)[None, :]
    ).astype(jnp.float32)
    live_slots = (jnp.arange(slot_count, dtype=jnp.int32) < near_live[0]).astype(jnp.float32)
    weights = jnp.dot(scale_pick, scale_table, precision=HIGHEST) * live_slots

    def apply_operator(values):
        own_values = values.astype(jnp.bfloat16)
        group_values = lax.all_gather(own_values, "dev", axis=1, tiled=True)
        near_part, far_part = operator_parts(
            group_values,
            own_values,
            near_blocks,
            near_rows,
            near_cols,
            weights,
            leaf_basis,
            leaf_transfer,
            device_transfer,
            device_coupling,
            group_coupling,
        )
        result = (
            0.5 * values
            + lax.psum_scatter(near_part, "dev", scatter_dimension=1, tiled=True)
            + far_part
        )
        return result

    basis_one, start_factor = orthonormal(start, total_panels)
    product_one = apply_operator(basis_one)
    basis_two, first_projections, factor_one = next_block(product_one, [basis_one], total_panels)
    product_two = apply_operator(basis_two)
    next_basis, second_projections, factor_two = next_block(
        product_two, [basis_one, basis_two], total_panels
    )
    hessenberg = jnp.stack(
        [first_projections[0], factor_one, second_projections[0], second_projections[1], factor_two]
    )
    return (next_basis, hessenberg)


def solution(mesh):
    placed = (
        P(None, ("grp", "dev")),
        P(("grp", "dev"), None, None),
        P(("grp", "dev")),
        P(("grp", "dev")),
        P(("grp", "dev")),
        P(),
        P(("grp", "dev")),
        P(("grp", "dev"), None, None),
        P(("grp", "dev"), None, None),
        P(("grp", "dev"), None, None),
        P(),
        P(),
    )
    return jax.shard_map(
        shards,
        mesh=mesh,
        in_specs=placed,
        out_specs=(P(None, ("grp", "dev")), P()),
        check_vma=False,
    )
```

profile of v0, /device:TPU:1, one launch (start us, length us, event | category | flops | bytes accessed | tf_op | source)
XLA Modules:
  0.0 826.8 jit_solution(3533810585517512542)
XLA Ops:
  8.6 68.8 %psum.35 = f32[1,32,32]{1,2,0:T(8,128)S(1)} all-reduce(f32[1,32,32]{1,2,0:T(8,128)S(1)} %convolution_bitcast_fusion.18), channel_id=1, replica_groups=mesh['grp'=8,'dev'=16] {'grp','dev'}, use_global_device_ids=true, to_apply=%region_0.0 | all-reduce | flops 1024 | bytes 8192 | tf_op jit(solution)/shard_map/psum | solution.py:126
  90.0 36.8 %all-gather.15.cloned.1.call-done = bf16[32,32768]{1,0:T(8,128)(2,1)} async-done(((bf16[32,2048]{1,0:T(8,128)(2,1)}), bf16[32,32768]{1,0:T(8,128)(2,1)}) %all-gather.15.cloned.1.call-update) | async-done | bytes 2097168 | tf_op jit(solution)/shard_map/all_gather | solution.py:176
  127.7 3.4 collective-permute-start
  131.8 4.5 collective-permute-done
  143.3 12.5 %broadcast_multiply_fusion.3 = f32[160,32,256]{2,1,0:T(8,128)} fusion(f32[160]{0:T(256)S(1)} %compare_select_fusion.2, bf16[160,256,256]{2,1,0:T(8,128)(2,1)} %param.18, bf16[160,32,256]{2,1,0:T(8,128)(2,1)} %gather_fusion, pred[160]{0:T(512)(128)(4,1)S(1)} %compare_and_fusion.1), kind=kOutput, calls=%fused_computation.25 | convolution fusion | flops 673710080 | bytes 28836640 | tf_op jit(solution)/shard_map/kij,rkj->rki/dot_general | solution.py:49
  158.6 25.2 %scatter_fusion = f32[32,144,256]{2,0,1:T(8,128)} fusion(f32[32,144,256]{2,0,1:T(8,128)} %broadcast.110.clone, s32[160]{0:T(256)S(1)} %compare_select_fusion.1, f32[160,32,256]{2,1,0:T(8,128)} %broadcast_multiply_fusion.3), kind=kCustom, calls=%fused_computation.4 | custom fusion | flops 1310720 | bytes 15729280 | tf_op jit(solution)/shard_map/scatter-add | solution.py:57
  183.8 12.9 %broadcast_multiply_fusion.2 = f32[160,32,256]{2,1,0:T(8,128)} fusion(f32[160]{0:T(256)S(1)} %compare_select_fusion.2, bf16[160,256,256]{2,1,0:T(8,128)(2,1)} %param.18, bf16[160,32,256]{2,1,0:T(8,128)(2,1)S(1)} %copy-done.1, pred[160]{0:T(512)(128)(4,1)S(1)} %compare_and_fusion), kind=kOutput, calls=%fused_computation.24 | convolution fusion | flops 673710080 | bytes 28836640 | tf_op jit(solution)/shard_map/kij,rki->rkj/dot_general | solution.py:53
  196.7 25.0 %scatter_fusion.1 = f32[32,144,256]{2,0,1:T(8,128)} fusion(f32[32,144,256]{2,0,1:T(8,128)} %scatter_fusion, s32[160]{0:T(256)S(1)} %compare_select_fusion, f32[160,32,256]{2,1,0:T(8,128)} %broadcast_multiply_fusion.2), kind=kCustom, calls=%fused_computation.5 | custom fusion | flops 1310720 | bytes 15729280 | tf_op jit(solution)/shard_map/scatter-add | solution.py:57
  227.3 3.6 collective-permute-done.1
  236.3 20.5 %all-gather.6 = f32[16,64,32]{1,2,0:T(8,128)} all-gather(f32[1,64,32]{1,2,0:T(8,128)S(1)} %bitcast.255), channel_id=2, replica_groups=mesh['grp'=8,'dev'=16] {'dev'}, dimensions={0}, use_global_device_ids=true | all-gather | bytes 139264 | tf_op jit(solution)/shard_map/all_gather | solution.py:75
  256.8 3.5 collective-permute-start.3
  260.4 7.4 collective-permute-start.2
  269.1 18.7 %all-gather.7 = f32[16,64,32]{1,2,0:T(8,128)} all-gather(f32[1,64,32]{1,2,0:T(8,128)S(1)} %convolution_bitcast_fusion.10), channel_id=3, replica_groups=mesh['grp'=8,'dev'=16] {'dev'}, dimensions={0}, use_global_device_ids=true | all-gather | bytes 139264 | tf_op jit(solution)/shard_map/all_gather | solution.py:76
  288.8 17.4 %all-gather.8 = f32[8,64,32]{1,2,0:T(8,128)S(1)} all-gather(f32[1,64,32]{1,2,0:T(8,128)S(1)} %bitcast.257), channel_id=4, replica_groups=mesh['grp'=8,'dev'=16] {'grp'}, dimensions={0}, use_global_device_ids=true | all-gather | bytes 73728 | tf_op jit(solution)/shard_map/all_gather | solution.py:79
  315.7 64.4 %psum.36 = f32[1,32,32]{1,2,0:T(8,128)S(1)} all-reduce(f32[1,32,32]{1,2,0:T(8,128)S(1)} %convolution_bitcast_fusion.16), channel_id=1, replica_groups=mesh['grp'=8,'dev'=16] {'grp','dev'}, use_global_device_ids=true, to_apply=%region_7.0 | all-reduce | flops 1024 | bytes 8192 | tf_op jit(solution)/shard_map/psum | solution.py:126
  381.8 64.2 %psum.37 = f32[1,32,32]{1,2,0:T(8,128)S(1)} all-reduce(f32[1,32,32]{1,2,0:T(8,128)S(1)} %convolution_bitcast_fusion.15), channel_id=1, replica_groups=mesh['grp'=8,'dev'=16] {'grp','dev'}, use_global_device_ids=true, to_apply=%region_8.0 | all-reduce | flops 1024 | bytes 8192 | tf_op jit(solution)/shard_map/psum | solution.py:126
  453.9 40.5 %all-gather.17.cloned.1.call-done = bf16[32,32768]{1,0:T(8,128)(2,1)} async-done(((bf16[32,2048]{1,0:T(8,128)(2,1)}), bf16[32,32768]{1,0:T(8,128)(2,1)}) %all-gather.17.cloned.1.call-update) | async-done | bytes 2097168 | tf_op jit(solution)/shard_map/all_gather | solution.py:176
  495.4 3.6 collective-permute-start.4
  499.0 5.2 collective-permute-done.4
  511.3 12.6 %broadcast_multiply_fusion.1 = f32[160,32,256]{2,1,0:T(8,128)} fusion(f32[160]{0:T(256)S(1)} %compare_select_fusion.2, bf16[160,256,256]{2,1,0:T(8,128)(2,1)} %param.18, bf16[160,32,256]{2,1,0:T(8,128)(2,1)} %gather_fusion.2, pred[160]{0:T(512)(128)(4,1)S(1)} %compare_and_fusion.1), kind=kOutput, calls=%fused_computation.23 | convolution fusion | flops 673710080 | bytes 28836640 | tf_op jit(solution)/shard_map/kij,rkj->rki/dot_general | solution.py:49
  523.9 13.0 %broadcast_multiply_fusion = f32[160,32,256]{2,1,0:T(8,128)} fusion(f32[160]{0:T(256)S(1)} %compare_select_fusion.2, bf16[160,256,256]{2,1,0:T(8,128)(2,1)} %param.18, bf16[160,32,256]{2,1,0:T(8,128)(2,1)S(1)} %copy-done.2, pred[160]{0:T(512)(128)(4,1)S(1)} %compare_and_fusion), kind=kOutput, calls=%fused_computation.22 | convolution fusion | flops 673710080 | bytes 28836640 | tf_op jit(solution)/shard_map/kij,rki->rkj/dot_general | solution.py:53
  539.8 25.1 %scatter_fusion.2 = f32[32,144,256]{2,0,1:T(8,128)} fusion(f32[32,144,256]{2,0,1:T(8,128)} %broadcast.110, s32[160]{0:T(256)S(1)} %compare_select_fusion.1, f32[160,32,256]{2,1,0:T(8,128)} %broadcast_multiply_fusion.1), kind=kCustom, calls=%fused_computation.6 | custom fusion | flops 1310720 | bytes 15729280 | tf_op jit(solution)/shard_map/scatter-add | solution.py:57
  564.8 25.1 %scatter_fusion.3 = f32[32,144,256]{2,0,1:T(8,128)} fusion(f32[32,144,256]{2,0,1:T(8,128)} %scatter_fusion.2, s32[160]{0:T(256)S(1)} %compare_select_fusion, f32[160,32,256]{2,1,0:T(8,128)} %broadcast_multiply_fusion), kind=kCustom, calls=%fused_computation.7 | custom fusion | flops 1310720 | bytes 15729280 | tf_op jit(solution)/shard_map/scatter-add | solution.py:57
  595.5 3.6 collective-permute-done.5
  604.5 19.0 %all-gather.9 = f32[16,64,32]{1,2,0:T(8,128)S(1)} all-gather(f32[1,64,32]{1,2,0:T(8,128)S(1)} %bitcast.256), channel_id=5, replica_groups=mesh['grp'=8,'dev'=16] {'dev'}, dimensions={0}, use_global_device_ids=true | all-gather | bytes 139264 | tf_op jit(solution)/shard_map/all_gather | solution.py:75
  623.5 3.1 collective-permute-start.7
  626.6 7.5 collective-permute-start.6
  634.4 17.6 %all-gather.10 = f32[16,64,32]{1,2,0:T(8,128)S(1)} all-gather(f32[1,64,32]{1,2,0:T(8,128)S(1)} %convolution_bitcast_fusion.8), channel_id=6, replica_groups=mesh['grp'=8,'dev'=16] {'dev'}, dimensions={0}, use_global_device_ids=true | all-gather | bytes 139264 | tf_op jit(solution)/shard_map/all_gather | solution.py:76
  652.1 16.8 %all-gather.11 = f32[8,64,32]{1,2,0:T(8,128)S(1)} all-gather(f32[1,64,32]{1,2,0:T(8,128)S(1)} %bitcast.258), channel_id=7, replica_groups=mesh['grp'=8,'dev'=16] {'grp'}, dimensions={0}, use_global_device_ids=true | all-gather | bytes 73728 | tf_op jit(solution)/shard_map/all_gather | solution.py:79
  672.9 6.9 reduce-scatter.5.cloned.1.call-done
  681.5 66.1 %psum.38 = f32[2,32,32]{2,1,0:T(8,128)S(1)} all-reduce(f32[2,32,32]{2,1,0:T(8,128)S(1)} %pad_maximum_fusion.3), channel_id=1, replica_groups=mesh['grp'=8,'dev'=16] {'grp','dev'}, use_global_device_ids=true, to_apply=%region_13.0 | all-reduce | flops 2048 | bytes 16384 | tf_op jit(solution)/shard_map/psum | solution.py:126
  748.8 62.6 %psum.39 = f32[1,32,32]{1,2,0:T(8,128)S(1)} all-reduce(f32[1,32,32]{1,2,0:T(8,128)S(1)} %convolution_bitcast_fusion.11), channel_id=1, replica_groups=mesh['grp'=8,'dev'=16] {'grp','dev'}, use_global_device_ids=true, to_apply=%region_14.18 | all-reduce | flops 1024 | bytes 8192 | tf_op jit(solution)/shard_map/psum | solution.py:126
  (143 shorter events, 94.2 us)
Async XLA Ops:
  7.2 228.3 %copy-start = (bf16[8,64,256]{2,1,0:T(8,128)(2,1)S(1)}, bf16[8,64,256]{2,1,0:T(8,128)(2,1)}, u32[]{:S(2)}) copy-start(bf16[8,64,256]{2,1,0:T(8,128)(2,1)} %param.24) | copy-start | bytes 786436
  7.2 119.6 %all-gather.15.cloned.1.call-start = ((), (), s32[]{:S(2)}) async-start(), calls=%async_computation.2 | async-start | bytes 2228224 | tf_op jit(solution)/shard_map/all_gather | solution.py:176
  86.3 228.1 %reduce-scatter.3.cloned.1.call-start = ((), (), s32[]{:S(2)}) async-start(), calls=%async_computation.3 | async-start | bytes 4456448 | tf_op jit(solution)/shard_map/reduce_scatter | solution.py:192
  127.7 8.6 %collective-permute-start = (bf16[32,4096]{1,0:T(8,128)(2,1)S(1)}, bf16[32,4096]{1,0:T(8,128)(2,1)S(1)}, u32[]{:S(2)}, u32[]{:S(2)}) collective-permute-start(bf16[32,4096]{1,0:T(8,128)(2,1)S(1)} %slice.55), channel_id=1, source_target_pairs={{16,0},{32,16},{48,32},{64,48},{80,64},{96,80},{112,96},{17,1},{33... | collective-permute-start | bytes 786440 | tf_op jit(solution)/shard_map/ppermute | solution.py:33
  158.6 25.2 %copy-start.1 = (bf16[160,32,256]{2,1,0:T(8,128)(2,1)S(1)}, bf16[160,32,256]{2,1,0:T(8,128)(2,1)}, u32[]{:S(2)}) copy-start(bf16[160,32,256]{2,1,0:T(8,128)(2,1)} %gather_fusion.1) | copy-start | bytes 7864324
  222.8 8.0 collective-permute-start.1
  234.9 0.9 copy-start.9
  234.9 1.1 copy-start.6
  234.9 33.0 %copy-start.11 = (f32[6,64,64]{2,1,0:T(8,128)S(1)}, f32[6,64,64]{2,1,0:T(8,128)}, u32[]{:S(2)}) copy-start(f32[6,64,64]{2,1,0:T(8,128)} %param.28) | copy-start | bytes 294916
  234.9 33.1 %copy-start.5 = (f32[30,64,64]{2,1,0:T(8,128)S(1)}, f32[30,64,64]{2,1,0:T(8,128)}, u32[]{:S(2)}) copy-start(f32[30,64,64]{2,1,0:T(8,128)} %param.27) | copy-start | bytes 1474564
  234.9 34.1 %copy-start.12 = (f32[1,64,64]{2,1,0:T(8,128)S(1)}, f32[1,64,64]{2,1,0:T(8,128)}, u32[]{:S(2)}) copy-start(f32[1,64,64]{2,1,0:T(8,128)} %param.26) | copy-start | bytes 49156
  234.9 259.5 %all-gather.17.cloned.1.call-start = ((), (), s32[]{:S(2)}) async-start(), calls=%async_computation.4 | async-start | bytes 2228224 | tf_op jit(solution)/shard_map/all_gather | solution.py:176
  256.8 53.0 %collective-permute-start.3 = (f32[16,64,32]{1,2,0:T(8,128)}, f32[16,64,32]{1,2,0:T(8,128)}, u32[]{:S(2)}, u32[]{:S(2)}) collective-permute-start(f32[16,64,32]{1,2,0:T(8,128)} %all-gather.6), channel_id=1, source_target_pairs={{16,0},{32,16},{48,32},{64,48},{80,64},{96,80},{112,96},{17,1},{33... | collective-permute-start | bytes 393224 | tf_op jit(solution)/shard_map/ppermute | solution.py:23
  260.4 49.4 %collective-permute-start.2 = (f32[16,64,32]{1,2,0:T(8,128)}, f32[16,64,32]{1,2,0:T(8,128)}, u32[]{:S(2)}, u32[]{:S(2)}) collective-permute-start(f32[16,64,32]{1,2,0:T(8,128)} %all-gather.6), channel_id=1, source_target_pairs={{0,16},{16,32},{32,48},{48,64},{64,80},{80,96},{96,112},{1,17},{17... | collective-permute-start | bytes 393224 | tf_op jit(solution)/shard_map/ppermute | solution.py:21
  306.9 6.9 copy-start.7
  309.6 1.2 copy-start.3
  453.9 225.9 %reduce-scatter.5.cloned.1.call-start = ((), (), s32[]{:S(2)}) async-start(), calls=%async_computation.5 | async-start | bytes 4456448 | tf_op jit(solution)/shard_map/reduce_scatter | solution.py:192
  495.4 8.8 %collective-permute-start.4 = (bf16[32,4096]{1,0:T(8,128)(2,1)S(1)}, bf16[32,4096]{1,0:T(8,128)(2,1)S(1)}, u32[]{:S(2)}, u32[]{:S(2)}) collective-permute-start(bf16[32,4096]{1,0:T(8,128)(2,1)S(1)} %slice.59), channel_id=1, source_target_pairs={{16,0},{32,16},{48,32},{64,48},{80,64},{96,80},{112,96},{17,1},{33... | collective-permute-start | bytes 786440 | tf_op jit(solution)/shard_map/ppermute | solution.py:33
  511.3 12.6 %copy-start.2 = (bf16[160,32,256]{2,1,0:T(8,128)(2,1)S(1)}, bf16[160,32,256]{2,1,0:T(8,128)(2,1)}, u32[]{:S(2)}) copy-start(bf16[160,32,256]{2,1,0:T(8,128)(2,1)} %gather_fusion.3) | copy-start | bytes 7864324
  591.0 8.0 collective-permute-start.5
  603.1 0.9 copy-start.10
  603.1 65.8 %copy-start.8 = (f32[8,64,64]{2,0,1:T(8,128)S(1)}, f32[8,64,64]{2,0,1:T(8,128)}, u32[]{:S(2)}) copy-start(f32[8,64,64]{2,0,1:T(8,128)} %copy-done.7) | copy-start | bytes 393220
  603.1 66.3 %copy-start.4 = (f32[48,64,64]{2,0,1:T(8,128)S(1)}, f32[48,64,64]{2,0,1:T(8,128)}, u32[]{:S(2)}) copy-start(f32[48,64,64]{2,0,1:T(8,128)} %copy-done.3) | copy-start | bytes 2359300
  623.5 45.9 %collective-permute-start.7 = (f32[16,64,32]{1,2,0:T(8,128)S(1)}, f32[16,64,32]{1,2,0:T(8,128)}, u32[]{:S(2)}, u32[]{:S(2)}) collective-permute-start(f32[16,64,32]{1,2,0:T(8,128)S(1)} %all-gather.9), channel_id=1, source_target_pairs={{16,0},{32,16},{48,32},{64,48},{80,64},{96,80},{112,96},{17,1},{33... | collective-permute-start | bytes 393224 | tf_op jit(solution)/shard_map/ppermute | solution.py:23
  626.6 42.8 %collective-permute-start.6 = (f32[16,64,32]{1,2,0:T(8,128)S(1)}, f32[16,64,32]{1,2,0:T(8,128)}, u32[]{:S(2)}, u32[]{:S(2)}) collective-permute-start(f32[16,64,32]{1,2,0:T(8,128)S(1)} %all-gather.9), channel_id=1, source_target_pairs={{0,16},{16,32},{32,48},{48,64},{64,80},{80,96},{96,112},{1,17},{17... | collective-permute-start | bytes 393224 | tf_op jit(solution)/shard_map/ppermute | solution.py:21
Sparse Core Ops, SparseCore 0:
  86.4 40.2 all-gather.14
  235.0 76.8 reduce-scatter.2
  454.0 40.3 all-gather.16
  603.2 76.4 reduce-scatter.4
where the time goes:
time: 838 us; the launch traced here: 827 us
  blocking collectives  436 us (52%)
  other arithmetic  133 us (16%)
  waiting for transfers between devices  101 us (12%)
  matrix products  74.7 us (9%)
  local copies, waits for them, and re-layouts  33.6 us (4%)
  starting transfers between devices  33.1 us (4%)
  between operations  15.4 us (2%)
    psum x5, blocking collectives, global_inner(): summed = lax.psum(stacked, ('grp', 'dev'))  326 us
    scatter-add x4, other arithmetic, near_window(): return totals.at[:, near_rows].add(to_rows).at[:, near_cols].add(to_columns)  100 us
    all_gather x2, waiting for transfers between devices, apply_operator(): group_values = lax.all_gather(own_values, 'dev', axis=1, tiled=True)  77.3 us
    all_gather x2, blocking collectives, far_field(): lax.all_gather(own_coeffs[None], 'dev', axis=0, tiled=True)  39.5 us
    all_gather x2, blocking collectives, far_field(): lax.all_gather(parent_part[None], 'dev', axis=0, tiled=True)  36.3 us
    all_gather x2, blocking collectives, far_field(): lax.all_gather(jnp.sum(group_parents, axis=0)[None], 'grp', axis=0, tiled...  34.2 us
    dot_general x2, matrix products, near_window(): jnp.einsum('kij,rki->rkj', near_blocks, row_values, preferred_element_typ...  25.9 us
    dot_general x2, matrix products, near_window(): jnp.einsum('kij,rkj->rki', near_blocks, column_values, preferred_element_...  25.1 us
  transfers between devices with their start and end apart: 12, of which 7 were waited for; matrix products, arithmetic and copies ran while one was open for 3% of the time, Pallas kernels for 0%

commit v1 on v0

v1 whole, which is shorter than its diff:
```python
import functools

import jax
import jax.numpy as jnp
from jax import lax
from jax.experimental import pallas as pl
from jax.experimental.pallas import tpu as pltpu
from jax.sharding import PartitionSpec as P

F32 = jnp.float32
BF16 = jnp.bfloat16
HIGHEST = lax.Precision.HIGHEST
MESH = pl.DeviceIdType.MESH

R = 32
K = 64
HALF = 128
ND = 16
NG = 8
CL = 8
NB = 160
NCL = ND * CL
WIN = NCL + 16
NOFF = 30
GOFF = 6
UNROLL = 16
NPAN = 262144

NN = (((1,), (0,)), ((), ()))
NT = (((1,), (1,)), ((), ()))


def dot(a, b, dims=NN):
    return lax.dot_general(a, b, dims, precision=HIGHEST, preferred_element_type=F32)


def bdot(a, b, dims=NN):
    return lax.dot_general(a, b, dims, preferred_element_type=F32)


def split(v):
    hi = v.astype(BF16)
    return hi, (v - hi.astype(F32)).astype(BF16)


def pack(v):
    return jnp.concatenate([v[0:8], v[8:16], v[16:24], v[24:32]], axis=1)


def unpack(v):
    return jnp.concatenate([v[:, 0:32], v[:, 32:64], v[:, 64:96], v[:, 96:128]], axis=0)


def factor(gram):
    row = lax.broadcasted_iota(jnp.int32, (R, R), 0)
    col = lax.broadcasted_iota(jnp.int32, (R, R), 1)
    eye = (row == col).astype(F32)
    rid = lax.broadcasted_iota(jnp.int32, (R, 1), 0)
    m = jnp.concatenate([gram, eye], axis=1)
    for k in range(R - 1):
        pivot = m[k : k + 1, :]
        inverse = 1.0 / m[k : k + 1, k : k + 1]
        scale = jnp.where(rid > k, m[:, k : k + 1] * inverse, 0.0)
        m = m - scale * pivot
    upper = m[:, :R]
    diag = jnp.sum(jnp.where(row == col, upper, 0.0), axis=1, keepdims=True)
    rs = 1.0 / jnp.sqrt(diag)
    lower = jnp.where(row <= col, upper * rs, 0.0).T
    return lower, jnp.where(row >= col, m[:, R:] * rs, 0.0)


def permuted(c):
    return jnp.where(c < NCL, ((c >> 3) & 3) * 32 + (c >> 5) * 8 + (c & 7), c)


NAMES = [
    "p1p", "p1m", "q0p", "q0m", "f1p", "f1m", "q1p", "q1m", "q2p", "q2m", "q3p", "q3m", "g0", "g1", "g2", "g3",
    "z0", "z1", "ov", "s1p", "s1m", "s2p", "s2m", "s3p", "s3m", "t1p", "t1m", "t2p", "t2m", "t3p", "t3m",
]
NUMBER = {(n, h): 2 * i + h for i, n in enumerate(NAMES) for h in range(2)}
QUP = 2 * len(NAMES)
QDN = QUP + 1
SEM_AR1 = QDN + 1
SEM_AR2 = SEM_AR1 + ND
SEM_FAR1 = SEM_AR2 + NG
SEM_FAR2 = SEM_FAR1 + ND
NSEM = SEM_FAR2 + NG


def kernel(
    rows, cols, scl, table, live, prev, last,
    start, lbasis, ltrans, dtrans, dcoup, gcoup, blocks_hbm,
    next_ref, hess_ref,
    blocks, seg, w0, w1, t0, t1, over, xbuf, ybuf, sbuf, ubuf, vbuf, mbuf, gbuf, ar1, ar2,
    ltcat, cah, cal, cbh, cbl, dah, dal, dbh, dbl, b1, b2, u, bsem, ssem, rsem,
):
    g = lax.axis_index("grp")
    d = lax.axis_index("dev")
    x, y = d // 4, d % 4
    w = (w0, w1)
    t = (t0, t1)
    ab = ((x, y), (y, x))

    def dev(h, a, b):
        return a * 4 + b if h == 0 else b * 4 + a

    def step(v, k):
        return (v + k) % 4

    near_copy = pltpu.make_async_copy(blocks_hbm, blocks, bsem.at[0])
    near_copy.start()

    def remote(src, dst, number, gg, dd):
        return pltpu.make_async_remote_copy(
            src_ref=src, dst_ref=dst, send_sem=ssem.at[number], recv_sem=rsem.at[number],
            device_id=(gg, dd), device_id_type=MESH,
        )

    mbuf[...] = jnp.zeros_like(mbuf)
    gbuf[...] = jnp.zeros_like(gbuf)
    over[...] = jnp.zeros_like(over)
    for h in range(2):
        w[h][NCL:WIN] = jnp.zeros((16, R, HALF), BF16)
    seg[2 * NB] = jnp.zeros((R, 2 * HALF), F32)

    barrier = pltpu.get_barrier_semaphore()

    def greet_dev(o, c):
        pl.semaphore_signal(barrier, inc=1, device_id=(g, (d + o) % ND), device_id_type=MESH)
        return c

    def greet_grp(o, c):
        pl.semaphore_signal(barrier, inc=1, device_id=((g + o) % NG, d), device_id_type=MESH)
        return c

    lax.fori_loop(1, ND, greet_dev, 0)
    lax.fori_loop(1, NG, greet_grp, 0)

    def all_reduce(i, parts, beside=None, first=False):
        n = 8 * len(parts)
        val = jnp.concatenate([pack(p) for p in parts], axis=0) if len(parts) > 1 else pack(parts[0])
        ar1[i, d, 0:n] = val
        if first:
            pl.semaphore_wait(barrier, ND + NG - 2)

        def along_dev(o):
            return remote(ar1.at[i, d, pl.ds(0, n)], ar1.at[i, d, pl.ds(0, n)], SEM_AR1 + o, g, (d + o) % ND)

        def along_grp(o):
            return remote(ar2.at[i, g, pl.ds(0, n)], ar2.at[i, g, pl.ds(0, n)], SEM_AR2 + o, (g + o) % NG, d)

        def go(make, count):
            lax.fori_loop(1, count, lambda o, c: (make(o).start(), c)[1], 0)

        def got(make, count):
            lax.fori_loop(1, count, lambda o, c: (make(o).wait_recv(), c)[1], 0)

        def left(make, count):
            lax.fori_loop(1, count, lambda o, c: (make(o).wait_send(), c)[1], 0)

        go(along_dev, ND)
        if beside is not None:
            beside()
        got(along_dev, ND)
        total = ar1[i, 0, 0:n]
        for e in range(1, ND):
            total = total + ar1[i, e, 0:n]
        ar2[i, g, 0:n] = total
        go(along_grp, NG)
        left(along_dev, ND)
        got(along_grp, NG)
        total = ar2[i, 0, 0:n]
        for e in range(1, NG):
            total = total + ar2[i, e, 0:n]
        left(along_grp, NG)
        total = total * (1.0 / NPAN)
        return [unpack(total[8 * j : 8 * j + 8]) for j in range(len(parts))]

    def tables():
        for i in range(CL // 2):
            ltcat[:, 128 * i : 128 * i + 128] = jnp.concatenate([ltrans[2 * i], ltrans[2 * i + 1]], axis=1)

        def build(src, count, ah, al, bh, bl):
            for i in range(count // 2):
                at = slice(128 * i, 128 * i + 128)
                ahead = jnp.concatenate([src[2 * i], src[2 * i + 1]], axis=1)
                ah[:, at], al[:, at] = split(ahead)
                o = count - 1 - 2 * i
                behind = jnp.concatenate([src[o], src[o - 1]], axis=0).T
                bh[:, at], bl[:, at] = split(behind)

        build(dcoup, NOFF, cah, cal, cbh, cbl)
        build(gcoup, GOFF, dah, dal, dbh, dbl)

    def far_send(i):
        return remote(
            mbuf.at[pl.ds((32 + d) * K, K)], mbuf.at[pl.ds((32 + d) * K, K)], SEM_FAR1 + i, g, (d + i) % ND
        )

    def top_send(i):
        return remote(gbuf.at[pl.ds((8 + g) * K, K)], gbuf.at[pl.ds((8 + g) * K, K)], SEM_FAR2 + i, (g + i) % NG, d)

    def apply(v_ref):
        vb = v_ref[...].astype(BF16)
        for h in range(2):
            for c in range(CL):
                lo = c * 256 + h * HALF
                w[h][(ab[h][0] * 4 + ab[h][1]) * CL + c] = vb[:, lo : lo + HALF]

        def ship(name, h, src, dst, dd, gg=None):
            c = remote(src, dst, NUMBER[name, h], g if gg is None else gg, dd)
            c.start()
            return c

        sent = []

        def shard(h, a, b, lo=0, n=CL):
            return w[h].at[pl.ds((a * 4 + b) * CL + lo, n)]

        def same(name, h, ref, dd):
            c = ship(name, h, ref, ref, dd)
            sent.append(c)
            return c

        cp = {}
        for h in range(2):
            a, b = ab[h]
            own = shard(h, a, b)
            cp["p1p", h] = same("p1p", h, own, dev(h, a, step(b, 1)))
            cp["p1m", h] = same("p1m", h, own, dev(h, a, step(b, 3)))
            cp["q0p", h] = same("q0p", h, own, dev(h, step(a, 1), b))
            cp["q0m", h] = same("q0m", h, own, dev(h, step(a, 3), b))

        q = jnp.concatenate([bdot(lbasis[c], vb[:, 256 * c : 256 * c + 256], NT) for c in range(CL)], axis=0)
        coeffs = dot(ltcat[...], q)
        parents = dot(dtrans[0], coeffs)
        qh, ql = split(coeffs)
        ph, pe = split(parents)
        mbuf[pl.ds(pl.multiple_of((32 + d) * K, K), K), :] = jnp.concatenate([qh, ql, ph, pe], axis=1)
        lax.fori_loop(1, ND, lambda o, c: (far_send(o).start(), c)[1], 0)

        for h in range(2):
            a, b = ab[h]
            cp["p1p", h].wait_recv()
            back = shard(h, a, step(b, 3))
            cp["f1p", h] = same("f1p", h, shard(h, a, step(b, 3), 0, 4), dev(h, a, step(b, 1)))
            cp["q1p", h] = same("q1p", h, back, dev(h, step(a, 1), b))
            cp["q1m", h] = same("q1m", h, back, dev(h, step(a, 3), b))
            cp["p1m", h].wait_recv()
            ahead = shard(h, a, step(b, 1))
            cp["f1m", h] = same("f1m", h, shard(h, a, step(b, 1), 4, 4), dev(h, a, step(b, 3)))
            cp["q2p", h] = same("q2p", h, ahead, dev(h, step(a, 1), b))
            cp["q2m", h] = same("q2m", h, ahead, dev(h, step(a, 3), b))
        for h in range(2):
            a, b = ab[h]
            cp["q0p", h].wait_recv()
            cp["g0", h] = same("g0", h, shard(h, step(a, 3), b), dev(h, step(a, 1), b))
            cp["q0m", h].wait_recv()
        for h in range(2):
            a, b = ab[h]
            cp["f1p", h].wait_recv()
            cp["f1m", h].wait_recv()
            across = shard(h, a, step(b, 2))
            cp["q3p", h] = same("q3p", h, across, dev(h, step(a, 1), b))
            cp["q3m", h] = same("q3m", h, across, dev(h, step(a, 3), b))

        lax.fori_loop(1, ND, lambda o, c: (far_send(o).wait_recv(), c)[1], 0)
        group_rows = pl.ds(32 * K, ND * K)
        up = remote(mbuf.at[group_rows], mbuf.at[pl.ds(16 * K, ND * K)], QUP, (g + 1) % NG, d)
        down = remote(mbuf.at[group_rows], mbuf.at[pl.ds(48 * K, ND * K)], QDN, (g + NG - 1) % NG, d)

        @pl.when(g < NG - 1)
        def _():
            up.start()

        @pl.when(g > 0)
        def _():
            down.start()

        top = mbuf[32 * K : 33 * K, :].astype(F32)
        for e in range(1, ND):
            top = top + mbuf[(32 + e) * K : (33 + e) * K, :].astype(F32)
        gh, gl = split(top[:, 64:96] + top[:, 96:128])
        gbuf[pl.ds(pl.multiple_of((8 + g) * K, K), K), :] = jnp.concatenate(
            [gh, gl, jnp.zeros((K, 64), BF16)], axis=1
        )
        lax.fori_loop(1, NG, lambda o, c: (top_send(o).start(), c)[1], 0)

        for h in range(2):
            a, b = ab[h]
            cp["q1p", h].wait_recv()
            cp["g1", h] = same("g1", h, shard(h, step(a, 3), step(b, 3)), dev(h, step(a, 1), b))
            cp["q1m", h].wait_recv()
            cp["q2m", h].wait_recv()
            cp["g2", h] = same("g2", h, shard(h, step(a, 1), step(b, 1)), dev(h, step(a, 3), b))
            cp["q2p", h].wait_recv()
        for h in range(2):
            a, b = ab[h]
            cp["q3m", h].wait_recv()
            cp["g3", h] = same("g3", h, shard(h, step(a, 1), step(b, 2)), dev(h, step(a, 3), b))
            cp["q3p", h].wait_recv()

        lax.fori_loop(1, NG, lambda o, c: (top_send(o).wait_recv(), c)[1], 0)

        @pl.when(g > 0)
        def _():
            up.wait_recv()

        @pl.when(g < NG - 1)
        def _():
            down.wait_recv()

        ga = gbuf[pl.ds(pl.multiple_of((10 + g) * K, K), GOFF * K), :]
        gb = gbuf[pl.ds(pl.multiple_of((1 + g) * K, K), GOFF * K), :]
        s1 = bdot(dah[...], ga) + bdot(dbh[...], gb)
        s2 = bdot(dal[...], ga) + bdot(dbl[...], gb)
        top_field = s1[:, 0:32] + s1[:, 32:64] + s2[:, 0:32]
        qa = mbuf[pl.ds(pl.multiple_of((34 + d) * K, K), NOFF * K), :]
        qb = mbuf[pl.ds(pl.multiple_of((1 + d) * K, K), NOFF * K), :]
        s1 = bdot(cah[...], qa) + bdot(cbh[...], qb)
        s2 = bdot(cal[...], qa) + bdot(cbl[...], qb)
        field = s1[:, 0:32] + s1[:, 32:64] + s2[:, 0:32]
        field_t = field.T + dot(top_field.T, dtrans[0])
        leaf_t = dot(field_t, ltcat[...])
        lh, ll = split(leaf_t)
        for c in range(CL):
            both = jnp.concatenate([lh[:, K * c : K * c + K], ll[:, K * c : K * c + K]], axis=0)
            far = bdot(both, lbasis[c])
            u[:, 256 * c : 256 * c + 256] = far[:R] + far[R:]

        for h in range(2):
            for n in ("g0", "g1", "g2", "g3"):
                cp[n, h].wait_recv()

        for h in range(2):
            for s in range(2):
                at = 4 if (h, s) == (1, 1) else s
                cp["z%d" % s, h] = remote(
                    w[h].at[pl.ds(at * CL, CL)], w[h].at[pl.ds(NCL + s * CL, CL)], NUMBER["z%d" % s, h], (g + NG - 1) % NG, d
                )

        @pl.when(g > 0)
        def _():
            for h in range(2):
                for s in range(2):
                    cp["z%d" % s, h].start()

        lax.fori_loop(1, ND, lambda o, c: (far_send(o).wait_send(), c)[1], 0)
        lax.fori_loop(1, NG, lambda o, c: (top_send(o).wait_send(), c)[1], 0)
        for c in sent:
            c.wait_send()

        @pl.when(g < NG - 1)
        def _():
            up.wait_send()
            for h in range(2):
                for s in range(2):
                    cp["z%d" % s, h].wait_recv()

        @pl.when(g > 0)
        def _():
            down.wait_send()

        n_live = live[0]

        def near(i, carry):
            for j in range(UNROLL):
                k = i * UNROLL + j
                r, c = rows[k], cols[k]
                weight = jnp.where(k < n_live, table[scl[k]], 0.0)
                block = blocks[k]
                vc = jnp.concatenate([w0[c], w1[permuted(c)]], axis=1)
                vr = jnp.concatenate([w0[r], w1[permuted(r)]], axis=1)
                to_row = bdot(block, vc, NT).T
                to_col = bdot(vr, block)
                seg[2 * k] = seg[prev[2 * k]] + weight * to_row
                seg[2 * k + 1] = seg[prev[2 * k + 1]] + weight * to_col
            return carry

        lax.fori_loop(0, NB // UNROLL, near, 0)

        @pl.when(g > 0)
        def _():
            for h in range(2):
                for s in range(2):
                    cp["z%d" % s, h].wait_send()

        for c in range(NCL, WIN):
            v = seg[last[c]]
            t0[c] = v[:, :HALF].astype(BF16)
            t1[c] = v[:, HALF:].astype(BF16)
        ov = [remote(t[h].at[pl.ds(NCL, 16)], over.at[h], NUMBER["ov", h], (g + 1) % NG, d) for h in range(2)]

        @pl.when(g < NG - 1)
        def _():
            for c in ov:
                c.start()

        def totals(i, carry):
            for j in range(CL):
                v = seg[last[i * CL + j]]
                t0[i * CL + j] = v[:, :HALF].astype(BF16)
                t1[(i % 4) * 32 + (i // 4) * CL + j] = v[:, HALF:].astype(BF16)
            return carry

        lax.fori_loop(2, ND, totals, 0)

        @pl.when(g > 0)
        def _():
            for c in ov:
                c.wait_recv()

        for i in range(2):
            for j in range(CL):
                v = seg[last[i * CL + j]]
                t0[i * CL + j] = (v[:, :HALF] + over[0, i * CL + j].astype(F32)).astype(BF16)
                t1[i * 32 + j] = (v[:, HALF:] + over[1, i * CL + j].astype(F32)).astype(BF16)

        sent.clear()

        def piece(h, a, lo):
            return t[h].at[pl.ds(a * 32 + lo, 16)]

        def to(name, h, src, dst, dd):
            cp[name, h] = ship(name, h, src, dst, dd)
            sent.append(cp[name, h])

        for h in range(2):
            a, b = ab[h]
            fwd, bwd = dev(h, step(a, 1), b), dev(h, step(a, 3), b)
            to("s1p", h, piece(h, step(a, 2), 0), xbuf.at[h, 0], fwd)
            to("s1m", h, piece(h, step(a, 2), 16), xbuf.at[h, 1], bwd)
            to("s2p", h, piece(h, step(a, 1), 16), ybuf.at[h, 0, pl.ds(16, 16)], fwd)
            to("s2m", h, piece(h, step(a, 3), 0), ybuf.at[h, 1, pl.ds(0, 16)], bwd)
        for h in range(2):
            a, b = ab[h]
            fwd, bwd = dev(h, step(a, 1), b), dev(h, step(a, 3), b)
            cp["s1p", h].wait_recv()
            at = pl.ds(step(a, 1) * 32, 16)
            t[h][at] = (t[h][at].astype(F32) + xbuf[h, 0].astype(F32)).astype(BF16)
            to("s3p", h, piece(h, step(a, 1), 0), ybuf.at[h, 0, pl.ds(0, 16)], fwd)
            cp["s1m", h].wait_recv()
            at = pl.ds(step(a, 3) * 32 + 16, 16)
            t[h][at] = (t[h][at].astype(F32) + xbuf[h, 1].astype(F32)).astype(BF16)
            to("s3m", h, piece(h, step(a, 3), 16), ybuf.at[h, 1, pl.ds(16, 16)], bwd)
        for h in range(2):
            a, b = ab[h]
            fwd, bwd = dev(h, a, step(b, 1)), dev(h, a, step(b, 3))
            for n in ("s2p", "s2m", "s3p", "s3m"):
                cp[n, h].wait_recv()
            for j in range(4):
                at = pl.ds(j * CL, CL)
                mine = t[h][pl.ds(a * 32 + j * CL, CL)].astype(F32)
                sbuf[h, at] = mine + ybuf[h, 0, at].astype(F32) + ybuf[h, 1, at].astype(F32)

            def part(k, lo):
                return sbuf.at[h, pl.ds(step(b, k) * CL + lo, 4)]

            to("t1p", h, part(2, 0), ubuf.at[h, 0], fwd)
            to("t1m", h, part(2, 4), ubuf.at[h, 1], bwd)
            to("t2p", h, part(1, 4), vbuf.at[h, 0, pl.ds(4, 4)], fwd)
            to("t2m", h, part(3, 0), vbuf.at[h, 1, pl.ds(0, 4)], bwd)
        for h in range(2):
            a, b = ab[h]
            fwd, bwd = dev(h, a, step(b, 1)), dev(h, a, step(b, 3))
            cp["t1p", h].wait_recv()
            at = pl.ds(step(b, 1) * CL, 4)
            sbuf[h, at] = sbuf[h, at] + ubuf[h, 0]
            to("t3p", h, sbuf.at[h, at], vbuf.at[h, 0, pl.ds(0, 4)], fwd)
            cp["t1m", h].wait_recv()
            at = pl.ds(step(b, 3) * CL + 4, 4)
            sbuf[h, at] = sbuf[h, at] + ubuf[h, 1]
            to("t3m", h, sbuf.at[h, at], vbuf.at[h, 1, pl.ds(4, 4)], bwd)
        for h in range(2):
            a, b = ab[h]
            for n in ("t2p", "t2m", "t3p", "t3m"):
                cp[n, h].wait_recv()
            for c in range(CL):
                total = sbuf[h, b * CL + c] + vbuf[h, 0, c] + vbuf[h, 1, c]
                lo = 256 * c + h * HALF
                u[:, lo : lo + HALF] = u[:, lo : lo + HALF] + total
        for c in sent:
            c.wait_send()

        @pl.when(g < NG - 1)
        def _():
            for c in ov:
                c.wait_send()

    row = lax.broadcasted_iota(jnp.int32, (R, R), 0)
    col = lax.broadcasted_iota(jnp.int32, (R, R), 1)
    half_eye = jnp.where(row == col, 0.5, 0.0)

    s = start[...]
    (gram,) = all_reduce(0, [dot(s, s, NT)], beside=tables, first=True)
    _, inverse = factor(gram)
    b1[...] = dot(inverse, s)
    near_copy.wait()
    apply(b1)

    uu = u[...]
    ha, gram = all_reduce(1, [dot(b1[...], uu, NT), dot(uu, uu, NT)])
    lower1, inverse = factor(gram - lax.dot_general(ha, ha, (((0,), (0,)), ((), ())), precision=HIGHEST))
    b2[...] = dot(inverse, uu) - dot(dot(inverse, ha, NT), b1[...])
    hess_ref[0] = ha + half_eye
    hess_ref[1] = lower1
    apply(b2)

    uu = u[...]
    hb, hc, gram = all_reduce(2, [dot(b1[...], uu, NT), dot(b2[...], uu, NT), dot(uu, uu, NT)])
    tn = (((0,), (0,)), ((), ()))
    gram = gram - dot(hb, hb, tn) - dot(hc, hc, tn)
    lower2, inverse = factor(gram)
    next_ref[...] = dot(inverse, uu) - dot(dot(inverse, hb, NT), b1[...]) - dot(dot(inverse, hc, NT), b2[...])
    hess_ref[2] = hb
    hess_ref[3] = hc + half_eye
    hess_ref[4] = lower2


def chains(near_rows, near_cols):
    target = jnp.stack([near_rows, near_cols], axis=1).reshape(-1)
    order = jnp.arange(2 * NB, dtype=jnp.int32)
    before = (target[:, None] == target[None, :]) & (order[None, :] < order[:, None])
    prev = jnp.max(jnp.where(before, order[None, :], -1), axis=1)
    hit = jnp.arange(WIN, dtype=jnp.int32)[:, None] == target[None, :]
    last = jnp.max(jnp.where(hit, order[None, :], -1), axis=1)
    return jnp.where(prev < 0, 2 * NB, prev), jnp.where(last < 0, 2 * NB, last)


def shards(
    start, near_blocks, near_rows, near_cols, near_scale, scale_table, near_live,
    leaf_basis, leaf_transfer, device_transfer, device_coupling, group_coupling,
):
    prev, last = chains(near_rows, near_cols)
    smem = pl.BlockSpec(memory_space=pltpu.SMEM)
    vmem = pl.BlockSpec(memory_space=pltpu.VMEM)
    return pl.pallas_call(
        kernel,
        out_shape=(jax.ShapeDtypeStruct((R, 2048), F32), jax.ShapeDtypeStruct((5, R, R), F32)),
        in_specs=[smem] * 7 + [vmem] * 6 + [pl.BlockSpec(memory_space=pl.ANY)],
        out_specs=(vmem, vmem),
        scratch_shapes=[
            pltpu.VMEM((NB, 256, 256), BF16),
            pltpu.VMEM((2 * NB + 1, R, 256), F32),
            pltpu.VMEM((WIN, R, HALF), BF16),
            pltpu.VMEM((WIN, R, HALF), BF16),
            pltpu.VMEM((WIN, R, HALF), BF16),
            pltpu.VMEM((WIN, R, HALF), BF16),
            pltpu.VMEM((2, 16, R, HALF), BF16),
            pltpu.VMEM((2, 2, 16, R, HALF), BF16),
            pltpu.VMEM((2, 2, 32, R, HALF), BF16),
            pltpu.VMEM((2, 32, R, HALF), F32),
            pltpu.VMEM((2, 2, 4, R, HALF), F32),
            pltpu.VMEM((2, 2, 8, R, HALF), F32),
            pltpu.VMEM((80 * K, 128), BF16),
            pltpu.VMEM((24 * K, 128), BF16),
            pltpu.VMEM((3, ND, 24, 128), F32),
            pltpu.VMEM((3, NG, 24, 128), F32),
            pltpu.VMEM((K, CL * K), F32),
            pltpu.VMEM((K, NOFF * K), BF16),
            pltpu.VMEM((K, NOFF * K), BF16),
            pltpu.VMEM((K, NOFF * K), BF16),
            pltpu.VMEM((K, NOFF * K), BF16),
            pltpu.VMEM((K, GOFF * K), BF16),
            pltpu.VMEM((K, GOFF * K), BF16),
            pltpu.VMEM((K, GOFF * K), BF16),
            pltpu.VMEM((K, GOFF * K), BF16),
            pltpu.VMEM((R, 2048), F32),
            pltpu.VMEM((R, 2048), F32),
            pltpu.VMEM((R, 2048), F32),
            pltpu.SemaphoreType.DMA((1,)),
            pltpu.SemaphoreType.DMA((NSEM,)),
            pltpu.SemaphoreType.DMA((NSEM,)),
        ],
        compiler_params=pltpu.CompilerParams(
            collective_id=0, has_side_effects=True, vmem_limit_bytes=60 * 2**20
        ),
        name="arnoldi",
    )(
        near_rows, near_cols, near_scale, scale_table, near_live, prev, last,
        start, leaf_basis, leaf_transfer, device_transfer, device_coupling, group_coupling, near_blocks,
    )


def solution(mesh):
    both = ("grp", "dev")
    cut = P(both, None, None)
    return jax.shard_map(
        shards,
        mesh=mesh,
        in_specs=(P(None, both), cut, P(both), P(both), P(both), P(), P(both), cut, cut, cut, P(), P()),
        out_specs=(P(None, both), P()),
        check_vma=False,
    )
```

time: 838 us -> 171 us (0.20); the launches traced: 827 us -> 171 us
  blocking collectives: 436 us -> 0 us
  Pallas kernels: 0 us -> 164 us
  other arithmetic: 133 us -> 2.21 us
  waiting for transfers between devices: 101 us -> 0 us
  matrix products: 74.7 us -> 0 us
  starting transfers between devices: 33.1 us -> 0 us
  local copies, waits for them, and re-layouts: 33.6 us -> 3.45 us
  between operations: 15.4 us -> 1.3 us
    psum x5 -> x0, blocking collectives: 326 us -> none  [global_inner(): summed = lax.psum(stacked, ('grp', 'dev'))]
    pallas_call x0 -> x1, Pallas kernels: none -> 164 us  [shards(): pl.pallas_call(kernel, out_shape=(jax.ShapeDtypeStruct((R, 2048), F32), j...]
    all_gather x6 -> x0, blocking collectives: 110 us -> none  [the longest x2 39.5 us: far_field(): lax.all_gather(own_coeffs[None], 'dev', axis=0, tiled=True)]
    scatter-add x4 -> x0, other arithmetic: 100 us -> none  [near_window(): return totals.at[:, near_rows].add(to_rows).at[:, near_cols].add(to_columns)]
    all_gather x2 -> x0, waiting for transfers between devices: 77.3 us -> none  [apply_operator(): group_values = lax.all_gather(own_values, 'dev', axis=1, tiled=True)]
    dot_general x34 -> x0, matrix products: 70.4 us -> none  [the longest x2 25.9 us: near_window(): jnp.einsum('kij,rki->rkj', near_blocks, row_values, preferred_element_typ...]
    ppermute x8 -> x0, starting transfers between devices: 32.5 us -> none  [the longest x2 15 us: extended(): lax.ppermute(tail, axis, [(i, (i + 1) % count) for i in range(ends)])]
    another operation x17 -> x1, other arithmetic: 20.7 us -> 0.71 us  [chains(): target = jnp.stack([near_rows, near_cols], axis=1).reshape(-1)]
  transfers between devices with their start and end apart: 12 -> 0, of which waited for: 7 -> 0; matrix products, arithmetic and copies ran while one was open for 3% -> 0% of each run, Pallas kernels for 0% -> 0%
where the time goes in v1:
time: 171 us
  Pallas kernels  164 us (96%)
  local copies, waits for them, and re-layouts  3.45 us (2%)
  other arithmetic  2.21 us (1%)
    pallas_call x1, Pallas kernels, shards(): pl.pallas_call(kernel, out_shape=(jax.ShapeDtypeStruct((R, 2048), F32), j...  164 us

profile of v1, /device:TPU:1, one launch (start us, length us, event | category | flops | bytes accessed | tf_op | source)
XLA Modules:
  0.0 171.0 jit_solution(9257144204854100634)
XLA Ops:
  1.3 0.7 pad_add_fusion
  2.0 0.1 copy.15
  2.1 0.1 eq.28
  2.2 0.1 select_reduce_fusion.1
  2.4 0.2 select_reduce_fusion
  2.6 0.6 compare_select_fusion.prev
  3.2 0.6 compare_select_fusion.1.last
  3.8 164.1 %arnoldi.1 = (f32[32,2048]{1,0:T(8,128)}, f32[5,32,32]{2,1,0:T(8,128)}) custom-call(s32[160]{0:T(256)} %rows.1, s32[160]{0:T(256)} %cols.1, s32[160]{0:T(256)} %scl.1, f32[256]{0:T(256)} %table.1, s32[1]{0:T(128)S(6)} %copy.18.live, s32[320]{0:T(512)} %compare_select_fusion.prev, s32[144]{0:T(256)} %compare_select_fusion.1.last, f32[32,2048]{1,0:T(8,128)} %start.1, ...), custom_call_target="tpu_custom_call" | custom-call | tf_op jit(solution)/shard_map/arnoldi/pallas_call | solution.py:537
  167.8 1.7 copy.19
  169.5 1.5 copy.20

commit v2 on v1

v2 whole, which is shorter than its diff:
```python
import functools

import jax
import jax.numpy as jnp
from jax import lax
from jax.experimental import pallas as pl
from jax.experimental.pallas import tpu as pltpu
from jax.sharding import PartitionSpec as P

F32 = jnp.float32
BF16 = jnp.bfloat16
HIGHEST = lax.Precision.HIGHEST
MESH = pl.DeviceIdType.MESH

R = 32
K = 64
HALF = 128
ND = 16
NG = 8
CL = 8
NB = 160
NCL = ND * CL
WIN = NCL + 16
NOFF = 30
GOFF = 6
UNROLL = 16
NPAN = 262144

NN = (((1,), (0,)), ((), ()))
NT = (((1,), (1,)), ((), ()))


def dot(a, b, dims=NN):
    return lax.dot_general(a, b, dims, precision=HIGHEST, preferred_element_type=F32)


def bdot(a, b, dims=NN):
    return lax.dot_general(a, b, dims, preferred_element_type=F32)


def split(v):
    hi = v.astype(BF16)
    return hi, (v - hi.astype(F32)).astype(BF16)


def terms(v):
    hi = v.astype(BF16)
    rest = v - hi.astype(F32)
    mid = rest.astype(BF16)
    return jnp.concatenate([hi, mid, (rest - mid.astype(F32)).astype(BF16)], axis=0)


def inner(a, b):
    p = bdot(a, b, NT)
    at = [slice(0, R), slice(R, 2 * R), slice(2 * R, 3 * R)]
    small = p[at[2], at[0]] + p[at[1], at[1]] + p[at[0], at[2]]
    return p[at[0], at[0]] + ((p[at[1], at[0]] + p[at[0], at[1]]) + small)


def combine(coeffs, blocks):
    parts = []
    for c in coeffs:
        hi = c.astype(BF16)
        rest = c - hi.astype(F32)
        mid = rest.astype(BF16)
        low = (rest - mid.astype(F32)).astype(BF16)
        zero = jnp.zeros((R, R), BF16)
        rows = [
            jnp.concatenate([hi, hi, hi], axis=1),
            jnp.concatenate([mid, mid, zero], axis=1),
            jnp.concatenate([low, zero, zero], axis=1),
        ]
        parts.append(jnp.concatenate(rows, axis=0))
    total = None
    for c, b in zip(parts, blocks):
        p = bdot(c, b)
        p = p[:R] + (p[R : 2 * R] + p[2 * R :])
        total = p if total is None else total + p
    return total


def pack(v):
    return jnp.concatenate([v[0:8], v[8:16], v[16:24], v[24:32]], axis=1)


def unpack(v):
    return jnp.concatenate([v[:, 0:32], v[:, 32:64], v[:, 64:96], v[:, 96:128]], axis=0)


def factor(gram):
    row = lax.broadcasted_iota(jnp.int32, (R, R), 0)
    col = lax.broadcasted_iota(jnp.int32, (R, R), 1)
    eye = (row == col).astype(F32)
    rid = lax.broadcasted_iota(jnp.int32, (R, 1), 0)
    m = jnp.concatenate([gram, eye], axis=1)
    for k in range(R - 1):
        pivot = m[k : k + 1, :]
        inverse = 1.0 / m[k : k + 1, k : k + 1]
        scale = jnp.where(rid > k, m[:, k : k + 1] * inverse, 0.0)
        m = m - scale * pivot
    upper = m[:, :R]
    diag = jnp.sum(jnp.where(row == col, upper, 0.0), axis=1, keepdims=True)
    rs = 1.0 / jnp.sqrt(diag)
    lower = jnp.where(row <= col, upper * rs, 0.0).T
    return lower, jnp.where(row >= col, m[:, R:] * rs, 0.0)


def permuted(c):
    return jnp.where(c < NCL, ((c >> 3) & 3) * 32 + (c >> 5) * 8 + (c & 7), c)


def num_p(h, o):
    return h * 3 + o - 1


def num_q(h, oa, j):
    return 6 + h * 12 + (oa - 1) * 4 + j


def num_z(h, s):
    return 30 + h * 2 + s


def num_ov(h):
    return 34 + h


def num_r(h, oa, j):
    return 36 + h * 12 + (oa - 1) * 4 + j


def num_v(h, o):
    return 60 + h * 3 + o - 1


QUP = 66
QDN = 67
SEM_AR1 = QDN + 1
SEM_AR2 = SEM_AR1 + ND
SEM_FAR1 = SEM_AR2 + NG
SEM_FAR2 = SEM_FAR1 + ND
NSEM = SEM_FAR2 + NG


def kernel(
    rows, cols, scl, table, live, prev, last,
    start_hbm, lbasis_hbm, ltrans_hbm, dtrans_hbm, dcoup_hbm, gcoup_hbm, blocks_hbm,
    next_ref, hess_ref,
    blocks, seg, w0, w1, t0, t1, over, ybuf, sbuf, vbuf, mbuf, gbuf, ar1, ar2,
    start, lbasis, ltrans, dtrans, dcoup, gcoup, ltcat, cah, cal, cbh, cbl, dah, dal, dbh, dbl, b1s, b2s, u, bsem, ssem, rsem,
):
    g = lax.axis_index("grp")
    d = lax.axis_index("dev")
    x, y = d // 4, d % 4
    w = (w0, w1)
    t = (t0, t1)
    ab = ((x, y), (y, x))

    def dev(h, a, b):
        return a * 4 + b if h == 0 else b * 4 + a

    def step(v, k):
        return (v + k) % 4

    pairs = (
        (start_hbm, start), (blocks_hbm, blocks), (dcoup_hbm, dcoup), (gcoup_hbm, gcoup),
        (ltrans_hbm, ltrans), (lbasis_hbm, lbasis), (dtrans_hbm, dtrans),
    )
    loads = [pltpu.make_async_copy(src, dst, bsem.at[i]) for i, (src, dst) in enumerate(pairs)]
    for i in (0, 2, 3, 4, 5, 6):
        loads[i].start()

    def remote(src, dst, number, gg, dd):
        return pltpu.make_async_remote_copy(
            src_ref=src, dst_ref=dst, send_sem=ssem.at[number], recv_sem=rsem.at[number],
            device_id=(gg, dd), device_id_type=MESH,
        )

    mbuf[...] = jnp.zeros_like(mbuf)
    gbuf[...] = jnp.zeros_like(gbuf)
    over[...] = jnp.zeros_like(over)
    for h in range(2):
        w[h][NCL:WIN] = jnp.zeros((16, R, HALF), BF16)
    seg[2 * NB] = jnp.zeros((R, 2 * HALF), F32)

    barrier = pltpu.get_barrier_semaphore()

    def greet_dev(o, c):
        pl.semaphore_signal(barrier, inc=1, device_id=(g, (d + o) % ND), device_id_type=MESH)
        return c

    def greet_grp(o, c):
        pl.semaphore_signal(barrier, inc=1, device_id=((g + o) % NG, d), device_id_type=MESH)
        return c

    lax.fori_loop(1, ND, greet_dev, 0)
    lax.fori_loop(1, NG, greet_grp, 0)

    def all_reduce(i, parts, beside=None, first=False):
        n = 8 * len(parts)
        val = jnp.concatenate([pack(p) for p in parts], axis=0) if len(parts) > 1 else pack(parts[0])
        ar1[i, d, 0:n] = val
        if first:
            pl.semaphore_wait(barrier, ND + NG - 2)

        def along_dev(o):
            return remote(ar1.at[i, d, pl.ds(0, n)], ar1.at[i, d, pl.ds(0, n)], SEM_AR1 + o, g, (d + o) % ND)

        def along_grp(o):
            return remote(ar2.at[i, g, pl.ds(0, n)], ar2.at[i, g, pl.ds(0, n)], SEM_AR2 + o, (g + o) % NG, d)

        def go(make, count):
            lax.fori_loop(1, count, lambda o, c: (make(o).start(), c)[1], 0)

        def got(make, count):
            lax.fori_loop(1, count, lambda o, c: (make(o).wait_recv(), c)[1], 0)

        def left(make, count):
            lax.fori_loop(1, count, lambda o, c: (make(o).wait_send(), c)[1], 0)

        go(along_dev, ND)
        if beside is not None:
            beside()
        got(along_dev, ND)
        total = ar1[i, 0, 0:n]
        for e in range(1, ND):
            total = total + ar1[i, e, 0:n]
        ar2[i, g, 0:n] = total
        go(along_grp, NG)
        left(along_dev, ND)
        got(along_grp, NG)
        total = ar2[i, 0, 0:n]
        for e in range(1, NG):
            total = total + ar2[i, e, 0:n]
        left(along_grp, NG)
        total = total * (1.0 / NPAN)
        return [unpack(total[8 * j : 8 * j + 8]) for j in range(len(parts))]

    def tables():
        loads[1].start()
        for i in range(2, 7):
            loads[i].wait()
        for i in range(CL // 2):
            ltcat[:, 128 * i : 128 * i + 128] = jnp.concatenate([ltrans[2 * i], ltrans[2 * i + 1]], axis=1)

        def build(src, count, ah, al, bh, bl):
            for i in range(count // 2):
                at = slice(128 * i, 128 * i + 128)
                ahead = jnp.concatenate([src[2 * i], src[2 * i + 1]], axis=1)
                ah[:, at], al[:, at] = split(ahead)
                o = count - 1 - 2 * i
                behind = jnp.concatenate([src[o], src[o - 1]], axis=0).T
                bh[:, at], bl[:, at] = split(behind)

        build(dcoup, NOFF, cah, cal, cbh, cbl)
        build(gcoup, GOFF, dah, dal, dbh, dbl)

    def far_send(i):
        return remote(
            mbuf.at[pl.ds((32 + d) * K, K)], mbuf.at[pl.ds((32 + d) * K, K)], SEM_FAR1 + i, g, (d + i) % ND
        )

    def top_send(i):
        return remote(gbuf.at[pl.ds((8 + g) * K, K)], gbuf.at[pl.ds((8 + g) * K, K)], SEM_FAR2 + i, (g + i) % NG, d)

    def shard(h, a, b):
        return w[h].at[pl.ds((a * 4 + b) * CL, CL)]

    def first(h, s):
        return (0, s) if h == 0 else (s, 0)

    def send_p(h, o):
        a, b = ab[h]
        return remote(shard(h, a, b), shard(h, a, b), num_p(h, o), g, dev(h, a, step(b, o)))

    def send_q(h, oa, j):
        a, b = ab[h]
        ref = shard(h, a, step(b, j))
        return remote(ref, ref, num_q(h, oa, j), g, dev(h, step(a, oa), b))

    def send_z(h, s):
        a, b = first(h, s)
        return remote(shard(h, a, b), w[h].at[pl.ds(NCL + s * CL, CL)], num_z(h, s), (g + NG - 1) % NG, d)

    def send_ov(h):
        return remote(t[h].at[pl.ds(NCL, 16)], over.at[h], num_ov(h), (g + 1) % NG, d)

    def send_r(h, oa, j):
        a, b = ab[h]
        src = t[h].at[pl.ds((step(a, oa) * 4 + step(b, j)) * CL, CL)]
        return remote(src, ybuf.at[h, oa - 1, j], num_r(h, oa, j), g, dev(h, step(a, oa), b))

    def send_v(h, o):
        a, b = ab[h]
        return remote(sbuf.at[h, o], vbuf.at[h, o - 1], num_v(h, o), g, dev(h, a, step(b, o)))

    def apply(v, first_call=False):
        vb = v.astype(BF16)
        for h in range(2):
            for c in range(CL):
                lo = c * 256 + h * HALF
                w[h][(ab[h][0] * 4 + ab[h][1]) * CL + c] = vb[:, lo : lo + HALF]

        for o in (1, 3, 2):
            for h in range(2):
                send_p(h, o).start()
        for oa in (1, 3, 2):
            for h in range(2):
                send_q(h, oa, 0).start()

        q = jnp.concatenate([bdot(lbasis[c], vb[:, 256 * c : 256 * c + 256], NT) for c in range(CL)], axis=0)
        coeffs = dot(ltcat[...], q)
        parents = dot(dtrans[0], coeffs)
        qh, ql = split(coeffs)
        ph, pe = split(parents)
        mbuf[pl.ds(pl.multiple_of((32 + d) * K, K), K), :] = jnp.concatenate([qh, ql, ph, pe], axis=1)

        for c in range(4):
            for h in range(2):
                b = ab[h][1]

                @pl.when(b != c)
                def _():
                    send_p(h, step(b, 4 - c)).wait_recv()
                    for oa in (1, 3, 2):
                        send_q(h, oa, step(c + 4 - b, 0)).start()

        for h in range(2):
            for s in range(2):
                sa, sb = first(h, s)
                a, b = ab[h]

                @pl.when(a != sa)
                def _():
                    send_q(h, step(a, 4 - sa), step(sb + 4 - b, 0)).wait_recv()

                @pl.when(g > 0)
                def _():
                    send_z(h, s).start()

        for h in range(2):
            a, b = ab[h]
            for oa in (1, 3, 2):
                for j in range(4):
                    from_a, from_b = step(a, 4 - oa), step(b, j)
                    if h == 0:
                        early = (from_a == 0) & (from_b < 2)
                    else:
                        early = (from_b == 0) & (from_a < 2)

                    @pl.when(jnp.logical_not(early))
                    def _():
                        send_q(h, oa, j).wait_recv()

        @pl.when(g < NG - 1)
        def _():
            for h in range(2):
                for s in range(2):
                    send_z(h, s).wait_recv()

        if first_call:
            loads[1].wait()

        lax.fori_loop(1, ND, lambda o, c: (far_send(o).start(), c)[1], 0)

        n_live = live[0]

        def near(i, carry):
            for j in range(UNROLL):
                k = i * UNROLL + j
                r, c = rows[k], cols[k]
                weight = jnp.where(k < n_live, table[scl[k]], 0.0)
                block = blocks[k]
                vc = jnp.concatenate([w0[c], w1[permuted(c)]], axis=1)
                vr = jnp.concatenate([w0[r], w1[permuted(r)]], axis=1)
                to_row = bdot(block, vc, NT).T
                to_col = bdot(vr, block)
                seg[2 * k] = seg[prev[2 * k]] + weight * to_row
                seg[2 * k + 1] = seg[prev[2 * k + 1]] + weight * to_col
            return carry

        lax.fori_loop(0, NB // UNROLL, near, 0)

        for h in range(2):
            for o in range(1, 4):
                send_p(h, o).wait_send()
                for j in range(4):
                    send_q(h, o, j).wait_send()

        @pl.when(g > 0)
        def _():
            for h in range(2):
                for s in range(2):
                    send_z(h, s).wait_send()

        for c in range(NCL, WIN):
            v = seg[last[c]]
            t0[c] = v[:, :HALF].astype(BF16)
            t1[c] = v[:, HALF:].astype(BF16)

        @pl.when(g < NG - 1)
        def _():
            for h in range(2):
                send_ov(h).start()

        def emit(i, extra):
            place = ((i // 4, i % 4), (i % 4, i // 4))
            vals = [seg[last[i * CL + c]] for c in range(CL)]
            for h in range(2):
                a, b = ab[h]
                oa, j = step(place[h][0] + 4 - a, 0), step(place[h][1] + 4 - b, 0)
                at = (place[h][0] * 4 + place[h][1]) * CL
                parts = [v[:, h * HALF : h * HALF + HALF] for v in vals]
                if extra:
                    parts = [p + over[h, i * CL + c].astype(F32) for c, p in enumerate(parts)]

                @pl.when(oa == 0)
                def _():
                    for c in range(CL):
                        sbuf[h, j, c] = parts[c]

                @pl.when(oa != 0)
                def _():
                    for c in range(CL):
                        t[h][at + c] = parts[c].astype(BF16)
                    send_r(h, oa, j).start()

        def totals(dx, dy):
            i = step(x, dx) * 4 + step(y, dy)

            @pl.when(i >= 2)
            def _():
                emit(i, False)

            return 0

        lax.fori_loop(0, 9, lambda r, c: totals(1 + r // 3, 1 + r % 3), 0)
        lax.fori_loop(1, 4, lambda r, c: totals(r, 0), 0)
        lax.fori_loop(0, 4, lambda r, c: totals(0, r), 0)

        @pl.when(g > 0)
        def _():
            for h in range(2):
                send_ov(h).wait_recv()

        for i in range(2):
            emit(i, True)

        lax.fori_loop(1, ND, lambda o, c: (far_send(o).wait_recv(), c)[1], 0)
        group_rows = pl.ds(32 * K, ND * K)
        up = remote(mbuf.at[group_rows], mbuf.at[pl.ds(16 * K, ND * K)], QUP, (g + 1) % NG, d)
        down = remote(mbuf.at[group_rows], mbuf.at[pl.ds(48 * K, ND * K)], QDN, (g + NG - 1) % NG, d)

        @pl.when(g < NG - 1)
        def _():
            up.start()

        @pl.when(g > 0)
        def _():
            down.start()

        top = mbuf[32 * K : 33 * K, :].astype(F32)
        for e in range(1, ND):
            top = top + mbuf[(32 + e) * K : (33 + e) * K, :].astype(F32)
        gh, gl = split(top[:, 64:96] + top[:, 96:128])
        gbuf[pl.ds(pl.multiple_of((8 + g) * K, K), K), :] = jnp.concatenate(
            [gh, gl, jnp.zeros((K, 64), BF16)], axis=1
        )
        lax.fori_loop(1, NG, lambda o, c: (top_send(o).start(), c)[1], 0)

        for o in (1, 3, 2, 0):
            for h in range(2):
                for oa in (1, 3, 2):
                    send_r(h, oa, o).wait_recv()
                sbuf[h, o] = sbuf[h, o] + (
                    ybuf[h, 0, o].astype(F32) + ybuf[h, 1, o].astype(F32) + ybuf[h, 2, o].astype(F32)
                )
                if o:
                    send_v(h, o).start()
        lax.fori_loop(1, NG, lambda o, c: (top_send(o).wait_recv(), c)[1], 0)

        @pl.when(g > 0)
        def _():
            up.wait_recv()

        @pl.when(g < NG - 1)
        def _():
            down.wait_recv()

        ga = gbuf[pl.ds(pl.multiple_of((10 + g) * K, K), GOFF * K), :]
        gb = gbuf[pl.ds(pl.multiple_of((1 + g) * K, K), GOFF * K), :]
        s1 = bdot(dah[...], ga) + bdot(dbh[...], gb)
        s2 = bdot(dal[...], ga) + bdot(dbl[...], gb)
        top_field = s1[:, 0:32] + s1[:, 32:64] + s2[:, 0:32]
        qa = mbuf[pl.ds(pl.multiple_of((34 + d) * K, K), NOFF * K), :]
        qb = mbuf[pl.ds(pl.multiple_of((1 + d) * K, K), NOFF * K), :]
        s1 = bdot(cah[...], qa) + bdot(cbh[...], qb)
        s2 = bdot(cal[...], qa) + bdot(cbl[...], qb)
        field = s1[:, 0:32] + s1[:, 32:64] + s2[:, 0:32]
        field_t = field.T + dot(top_field.T, dtrans[0])
        leaf_t = dot(field_t, ltcat[...])
        lh, ll = split(leaf_t)
        for c in range(CL):
            both = jnp.concatenate([lh[:, K * c : K * c + K], ll[:, K * c : K * c + K]], axis=0)
            far = bdot(both, lbasis[c])
            u[:, 256 * c : 256 * c + 256] = far[:R] + far[R:]

        lax.fori_loop(1, ND, lambda o, c: (far_send(o).wait_send(), c)[1], 0)
        lax.fori_loop(1, NG, lambda o, c: (top_send(o).wait_send(), c)[1], 0)
        @pl.when(g < NG - 1)
        def _():
            up.wait_send()

        @pl.when(g > 0)
        def _():
            down.wait_send()

        for h in range(2):
            for o in (1, 3, 2):
                send_v(h, o).wait_recv()
            for c in range(CL):
                total = sbuf[h, 0, c] + vbuf[h, 0, c] + vbuf[h, 1, c] + vbuf[h, 2, c]
                lo = 256 * c + h * HALF
                u[:, lo : lo + HALF] = u[:, lo : lo + HALF] + total
        for h in range(2):
            for o in range(1, 4):
                send_v(h, o).wait_send()
                for j in range(4):
                    send_r(h, o, j).wait_send()

        @pl.when(g < NG - 1)
        def _():
            for h in range(2):
                send_ov(h).wait_send()

    row = lax.broadcasted_iota(jnp.int32, (R, R), 0)
    col = lax.broadcasted_iota(jnp.int32, (R, R), 1)
    half_eye = jnp.where(row == col, 0.5, 0.0)

    tn = (((0,), (0,)), ((), ()))
    loads[0].wait()
    ss = terms(start[...])
    (gram,) = all_reduce(0, [inner(ss, ss)], beside=tables, first=True)
    _, inverse = factor(gram)
    v = combine([inverse], [ss])
    b1s[...] = terms(v)
    apply(v, first_call=True)

    us = terms(u[...])
    ha, gram = all_reduce(1, [inner(b1s[...], us), inner(us, us)])
    lower1, inverse = factor(gram - dot(ha, ha, tn))
    v = combine([inverse, -dot(inverse, ha, NT)], [us, b1s[...]])
    b2s[...] = terms(v)
    hess_ref[0] = ha + half_eye
    hess_ref[1] = lower1
    apply(v)

    us = terms(u[...])
    hb, hc, gram = all_reduce(2, [inner(b1s[...], us), inner(b2s[...], us), inner(us, us)])
    lower2, inverse = factor(gram - dot(hb, hb, tn) - dot(hc, hc, tn))
    next_ref[...] = combine(
        [inverse, -dot(inverse, hb, NT), -dot(inverse, hc, NT)], [us, b1s[...], b2s[...]]
    )
    hess_ref[2] = hb
    hess_ref[3] = hc + half_eye
    hess_ref[4] = lower2


def chains(near_rows, near_cols):
    target = jnp.stack([near_rows, near_cols], axis=1).reshape(-1)
    order = jnp.arange(2 * NB, dtype=jnp.int32)
    before = (target[:, None] == target[None, :]) & (order[None, :] < order[:, None])
    prev = jnp.max(jnp.where(before, order[None, :], -1), axis=1)
    hit = jnp.arange(WIN, dtype=jnp.int32)[:, None] == target[None, :]
    last = jnp.max(jnp.where(hit, order[None, :], -1), axis=1)
    return jnp.where(prev < 0, 2 * NB, prev), jnp.where(last < 0, 2 * NB, last)


def shards(
    start, near_blocks, near_rows, near_cols, near_scale, scale_table, near_live,
    leaf_basis, leaf_transfer, device_transfer, device_coupling, group_coupling,
):
    prev, last = chains(near_rows, near_cols)
    smem = pl.BlockSpec(memory_space=pltpu.SMEM)
    vmem = pl.BlockSpec(memory_space=pltpu.VMEM)
    anywhere = pl.BlockSpec(memory_space=pltpu.HBM)
    outs = (jax.ShapeDtypeStruct((R, 2048), F32), jax.ShapeDtypeStruct((5, R, R), F32))
    return pl.pallas_call(
        kernel,
        out_shape=outs,
        in_specs=[smem] * 7 + [anywhere] * 7,
        out_specs=(vmem, vmem),
        scratch_shapes=[
            pltpu.VMEM((NB, 256, 256), BF16),
            pltpu.VMEM((2 * NB + 1, R, 256), F32),
            pltpu.VMEM((WIN, R, HALF), BF16),
            pltpu.VMEM((WIN, R, HALF), BF16),
            pltpu.VMEM((WIN, R, HALF), BF16),
            pltpu.VMEM((WIN, R, HALF), BF16),
            pltpu.VMEM((2, 16, R, HALF), BF16),
            pltpu.VMEM((2, 3, 4, CL, R, HALF), BF16),
            pltpu.VMEM((2, 4, CL, R, HALF), F32),
            pltpu.VMEM((2, 3, CL, R, HALF), F32),
            pltpu.VMEM((80 * K, 128), BF16),
            pltpu.VMEM((24 * K, 128), BF16),
            pltpu.VMEM((3, ND, 24, 128), F32),
            pltpu.VMEM((3, NG, 24, 128), F32),
            pltpu.VMEM((R, 2048), F32),
            pltpu.VMEM((CL, K, 256), BF16),
            pltpu.VMEM((CL, K, K), F32),
            pltpu.VMEM((1, K, K), F32),
            pltpu.VMEM((NOFF, K, K), F32),
            pltpu.VMEM((GOFF, K, K), F32),
            pltpu.VMEM((K, CL * K), F32),
            pltpu.VMEM((K, NOFF * K), BF16),
            pltpu.VMEM((K, NOFF * K), BF16),
            pltpu.VMEM((K, NOFF * K), BF16),
            pltpu.VMEM((K, NOFF * K), BF16),
            pltpu.VMEM((K, GOFF * K), BF16),
            pltpu.VMEM((K, GOFF * K), BF16),
            pltpu.VMEM((K, GOFF * K), BF16),
            pltpu.VMEM((K, GOFF * K), BF16),
            pltpu.VMEM((3 * R, 2048), BF16),
            pltpu.VMEM((3 * R, 2048), BF16),
            pltpu.VMEM((R, 2048), F32),
            pltpu.SemaphoreType.DMA((7,)),
            pltpu.SemaphoreType.DMA((NSEM,)),
            pltpu.SemaphoreType.DMA((NSEM,)),
        ],
        compiler_params=pltpu.CompilerParams(
            collective_id=0, has_side_effects=True, vmem_limit_bytes=60 * 2**20
        ),
        name="arnoldi",
    )(
        near_rows, near_cols, near_scale, scale_table, near_live, prev, last,
        start, leaf_basis, leaf_transfer, device_transfer, device_coupling, group_coupling, near_blocks,
    )


def solution(mesh):
    both = ("grp", "dev")
    cut = P(both, None, None)
    return jax.shard_map(
        shards,
        mesh=mesh,
        in_specs=(P(None, both), cut, P(both), P(both), P(both), P(), P(both), cut, cut, cut, P(), P()),
        out_specs=(P(None, both), P()),
        check_vma=False,
    )
```

time: 171 us -> 153 us (0.89)
  Pallas kernels: 164 us -> 146 us
    pallas_call x1, Pallas kernels: 164 us -> 146 us  [shards(): pl.pallas_call(kernel, out_shape=outs, in_specs=[smem] * 7 + [anywhere] *...]
where the time goes in v2:
time: 153 us
  Pallas kernels  146 us (95%)
  local copies, waits for them, and re-layouts  3.45 us (2%)
  other arithmetic  2.21 us (1%)
    pallas_call x1, Pallas kernels, shards(): pl.pallas_call(kernel, out_shape=outs, in_specs=[smem] * 7 + [anywhere] *...  146 us
    unnamed x2, local copies, waits for them, and re-layouts  3.2 us

profile of v2, /device:TPU:1, one launch (start us, length us, event | category | flops | bytes accessed | tf_op | source)
XLA Modules:
  0.0 152.6 jit_solution(7572930642353571675)
XLA Ops:
  1.3 0.7 pad_add_fusion
  2.0 0.1 copy.15
  2.1 0.1 eq.28
  2.2 0.1 select_reduce_fusion.1
  2.4 0.2 select_reduce_fusion
  2.6 0.6 compare_select_fusion.prev
  3.2 0.6 compare_select_fusion.1.last
  3.8 145.6 %arnoldi.1 = (f32[32,2048]{1,0:T(8,128)}, f32[5,32,32]{2,1,0:T(8,128)}) custom-call(s32[160]{0:T(256)} %rows.1, s32[160]{0:T(256)} %cols.1, s32[160]{0:T(256)} %scl.1, f32[256]{0:T(256)} %table.1, s32[1]{0:T(128)S(6)} %copy.18.live, s32[320]{0:T(512)} %compare_select_fusion.prev, s32[144]{0:T(256)} %compare_select_fusion.1.last, f32[32,2048]{1,0:T(8,128)} %start_hbm.1, ...), custom_call_target="tpu_custom_call" | custom-call | tf_op jit(solution)/shard_map/arnoldi/pallas_call | solution.py:588
  149.4 1.7 %copy.19 = f32[32,2048]{1,0:T(8,128)} copy(f32[32,2048]{1,0:T(8,128)} %get-tuple-element.4) | data formatting | bytes 524288
  151.1 1.5 %copy.20 = f32[5,32,32]{2,1,0:T(8,128)} copy(f32[5,32,32]{2,1,0:T(8,128)} %get-tuple-element.5) | data formatting | bytes 40960

commit v3 on v2

--- a/solution.py
+++ b/solution.py
@@ -13,6 +13,7 @@
 MESH = pl.DeviceIdType.MESH
 
 R = 32
+RB = 16
 K = 64
 HALF = 128
 ND = 16
@@ -109,32 +110,35 @@
     return jnp.where(c < NCL, ((c >> 3) & 3) * 32 + (c >> 5) * 8 + (c & 7), c)
 
 
-def num_p(h, o):
-    return h * 3 + o - 1
-
-
-def num_q(h, oa, j):
-    return 6 + h * 12 + (oa - 1) * 4 + j
-
-
-def num_z(h, s):
-    return 30 + h * 2 + s
-
-
-def num_ov(h):
-    return 34 + h
-
-
-def num_r(h, oa, j):
-    return 36 + h * 12 + (oa - 1) * 4 + j
-
-
-def num_v(h, o):
-    return 60 + h * 3 + o - 1
-
-
-QUP = 66
-QDN = 67
+PER = 66
+
+
+def num_p(p, h, o):
+    return p * PER + h * 3 + o - 1
+
+
+def num_q(p, h, oa, j):
+    return p * PER + 6 + h * 12 + (oa - 1) * 4 + j
+
+
+def num_z(p, h, s):
+    return p * PER + 30 + h * 2 + s
+
+
+def num_ov(p, h):
+    return p * PER + 34 + h
+
+
+def num_r(p, h, oa, j):
+    return p * PER + 36 + h * 12 + (oa - 1) * 4 + j
+
+
+def num_v(p, h, o):
+    return p * PER + 60 + h * 3 + o - 1
+
+
+QUP = 2 * PER
+QDN = QUP + 1
 SEM_AR1 = QDN + 1
 SEM_AR2 = SEM_AR1 + ND
 SEM_FAR1 = SEM_AR2 + NG
@@ -146,14 +150,15 @@
     rows, cols, scl, table, live, prev, last,
     start_hbm, lbasis_hbm, ltrans_hbm, dtrans_hbm, dcoup_hbm, gcoup_hbm, blocks_hbm,
     next_ref, hess_ref,
-    blocks, seg, w0, w1, t0, t1, over, ybuf, sbuf, vbuf, mbuf, gbuf, ar1, ar2,
+    blocks, segc, segr0, segr1, w00, w01, w10, w11, t00, t01, t10, t11, over, ybuf, sbuf, vbuf, mbuf, gbuf, ar1, ar2,
     start, lbasis, ltrans, dtrans, dcoup, gcoup, ltcat, cah, cal, cbh, cbl, dah, dal, dbh, dbl, b1s, b2s, u, bsem, ssem, rsem,
 ):
     g = lax.axis_index("grp")
     d = lax.axis_index("dev")
     x, y = d // 4, d % 4
-    w = (w0, w1)
-    t = (t0, t1)
+    segr = (segr0, segr1)
+    w = ((w00, w01), (w10, w11))
+    t = ((t00, t01), (t10, t11))
     ab = ((x, y), (y, x))
 
     def dev(h, a, b):
@@ -179,9 +184,11 @@
     mbuf[...] = jnp.zeros_like(mbuf)
     gbuf[...] = jnp.zeros_like(gbuf)
     over[...] = jnp.zeros_like(over)
-    for h in range(2):
-        w[h][NCL:WIN] = jnp.zeros((16, R, HALF), BF16)
-    seg[2 * NB] = jnp.zeros((R, 2 * HALF), F32)
+    for p in range(2):
+        for h in range(2):
+            w[p][h][NCL:WIN] = jnp.zeros((16, RB, HALF), BF16)
+        segr[p][NB] = jnp.zeros((R, HALF), F32)
+    segc[NB] = jnp.zeros((R, 2 * HALF), F32)
 
     barrier = pltpu.get_barrier_semaphore()
 
@@ -263,50 +270,204 @@
     def top_send(i):
         return remote(gbuf.at[pl.ds((8 + g) * K, K)], gbuf.at[pl.ds((8 + g) * K, K)], SEM_FAR2 + i, (g + i) % NG, d)
 
-    def shard(h, a, b):
-        return w[h].at[pl.ds((a * 4 + b) * CL, CL)]
+    def shard(p, h, a, b):
+        return w[p][h].at[pl.ds((a * 4 + b) * CL, CL)]
 
     def first(h, s):
         return (0, s) if h == 0 else (s, 0)
 
-    def send_p(h, o):
+    def send_p(p, h, o):
         a, b = ab[h]
-        return remote(shard(h, a, b), shard(h, a, b), num_p(h, o), g, dev(h, a, step(b, o)))
-
-    def send_q(h, oa, j):
+        return remote(shard(p, h, a, b), shard(p, h, a, b), num_p(p, h, o), g, dev(h, a, step(b, o)))
+
+    def send_q(p, h, oa, j):
         a, b = ab[h]
-        ref = shard(h, a, step(b, j))
-        return remote(ref, ref, num_q(h, oa, j), g, dev(h, step(a, oa), b))
-
-    def send_z(h, s):
+        ref = shard(p, h, a, step(b, j))
+        return remote(ref, ref, num_q(p, h, oa, j), g, dev(h, step(a, oa), b))
+
+    def send_z(p, h, s):
         a, b = first(h, s)
-        return remote(shard(h, a, b), w[h].at[pl.ds(NCL + s * CL, CL)], num_z(h, s), (g + NG - 1) % NG, d)
-
-    def send_ov(h):
-        return remote(t[h].at[pl.ds(NCL, 16)], over.at[h], num_ov(h), (g + 1) % NG, d)
-
-    def send_r(h, oa, j):
+        return remote(
+            shard(p, h, a, b), w[p][h].at[pl.ds(NCL + s * CL, CL)], num_z(p, h, s), (g + NG - 1) % NG, d
+        )
+
+    def send_ov(p, h):
+        return remote(t[p][h].at[pl.ds(NCL, 16)], over.at[p, h], num_ov(p, h), (g + 1) % NG, d)
+
+    def send_r(p, h, oa, j):
         a, b = ab[h]
-        src = t[h].at[pl.ds((step(a, oa) * 4 + step(b, j)) * CL, CL)]
-        return remote(src, ybuf.at[h, oa - 1, j], num_r(h, oa, j), g, dev(h, step(a, oa), b))
-
-    def send_v(h, o):
+        src = t[p][h].at[pl.ds((step(a, oa) * 4 + step(b, j)) * CL, CL)]
+        return remote(src, ybuf.at[p, h, oa - 1, j], num_r(p, h, oa, j), g, dev(h, step(a, oa), b))
+
+    def send_v(p, h, o):
         a, b = ab[h]
-        return remote(sbuf.at[h, o], vbuf.at[h, o - 1], num_v(h, o), g, dev(h, a, step(b, o)))
+        return remote(sbuf.at[p, h, o], vbuf.at[p, h, o - 1], num_v(p, h, o), g, dev(h, a, step(b, o)))
 
     def apply(v, first_call=False):
         vb = v.astype(BF16)
-        for h in range(2):
-            for c in range(CL):
-                lo = c * 256 + h * HALF
-                w[h][(ab[h][0] * 4 + ab[h][1]) * CL + c] = vb[:, lo : lo + HALF]
-
-        for o in (1, 3, 2):
+        for p in range(2):
             for h in range(2):
-                send_p(h, o).start()
-        for oa in (1, 3, 2):
+                for c in range(CL):
+                    lo = c * 256 + p * HALF
+                    w[p][h][(ab[h][0] * 4 + ab[h][1]) * CL + c] = vb[h * RB : h * RB + RB, lo : lo + HALF]
+
+        def along_b(p):
+            for o in (1, 3, 2):
+                for h in range(2):
+                    send_p(p, h, o).start()
+
+        def own_along_a(p):
+            for oa in (1, 3, 2):
+                for h in range(2):
+                    send_q(p, h, oa, 0).start()
+
+        def along_a(p):
+            for c in range(4):
+                for h in range(2):
+                    b = ab[h][1]
+
+                    @pl.when(b != c)
+                    def _():
+                        send_p(p, h, step(b, 4 - c)).wait_recv()
+                        for oa in (1, 3, 2):
+                            send_q(p, h, oa, step(c + 4 - b, 0)).start()
+
+        def pass_on(p):
             for h in range(2):
-                send_q(h, oa, 0).start()
+                for s in range(2):
+                    sa, sb = first(h, s)
+                    a, b = ab[h]
+
+                    @pl.when(a != sa)
+                    def _():
+                        send_q(p, h, step(a, 4 - sa), step(sb + 4 - b, 0)).wait_recv()
+
+                    @pl.when(g > 0)
+                    def _():
+                        send_z(p, h, s).start()
+
+        def gathered(p):
+            for h in range(2):
+                a, b = ab[h]
+                for oa in (1, 3, 2):
+                    for j in range(4):
+                        from_a, from_b = step(a, 4 - oa), step(b, j)
+                        if h == 0:
+                            early = (from_a == 0) & (from_b < 2)
+                        else:
+                            early = (from_b == 0) & (from_a < 2)
+
+                        @pl.when(jnp.logical_not(early))
+                        def _():
+                            send_q(p, h, oa, j).wait_recv()
+
+            @pl.when(g < NG - 1)
+            def _():
+                for h in range(2):
+                    for s in range(2):
+                        send_z(p, h, s).wait_recv()
+
+        n_live = live[0]
+
+        def panels(p, c):
+            return jnp.concatenate([w[p][0][c], w[p][1][permuted(c)]], axis=0)
+
+        def loop(one):
+            def some(i, carry):
+                for j in range(UNROLL):
+                    k = i * UNROLL + j
+                    one(k, jnp.where(k < n_live, table[scl[k]], 0.0))
+                return carry
+
+            lax.fori_loop(0, NB // UNROLL, some, 0)
+
+        def near_first(k, weight):
+            segc[k] = bdot(panels(0, rows[k]), blocks[k, 0:HALF])
+
+        def near_second(k, weight):
+            to_col = segc[k] + bdot(panels(1, rows[k]), blocks[k, HALF : 2 * HALF])
+            segc[k] = segc[prev[1, k]] + weight * to_col
+            near_row(0, k, weight)
+
+        def near_row(p, k, weight):
+            c = cols[k]
+            both = jnp.concatenate([panels(0, c), panels(1, c)], axis=1)
+            to_row = bdot(blocks[k, p * HALF : p * HALF + HALF], both, NT).T
+            segr[p][k] = segr[p][prev[0, k]] + weight * to_row
+
+        def near_total(p, c):
+            return segr[p][last[0, c]] + segc[last[1, c], :, p * HALF : p * HALF + HALF]
+
+        def emit(p, i, extra):
+            place = ((i // 4, i % 4), (i % 4, i // 4))
+            vals = [near_total(p, i * CL + c) for c in range(CL)]
+            for h in range(2):
+                a, b = ab[h]
+                oa, j = step(place[h][0] + 4 - a, 0), step(place[h][1] + 4 - b, 0)
+                at = (place[h][0] * 4 + place[h][1]) * CL
+                parts = [v[h * RB : h * RB + RB] for v in vals]
+                if extra:
+                    parts = [v + over[p, h, i * CL + c].astype(F32) for c, v in enumerate(parts)]
+
+                @pl.when(oa == 0)
+                def _():
+                    for c in range(CL):
+                        sbuf[p, h, j, c] = parts[c]
+
+                @pl.when(oa != 0)
+                def _():
+                    for c in range(CL):
+                        t[p][h][at + c] = parts[c].astype(BF16)
+                    send_r(p, h, oa, j).start()
+
+        def overflow(p):
+            for c in range(NCL, WIN):
+                v = near_total(p, c)
+                t[p][0][c] = v[:RB].astype(BF16)
+                t[p][1][c] = v[RB:].astype(BF16)
+
+            @pl.when(g < NG - 1)
+            def _():
+                for h in range(2):
+                    send_ov(p, h).start()
+
+        def totals(p):
+            def one(dx, dy):
+                i = step(x, dx) * 4 + step(y, dy)
+
+                @pl.when(i >= 2)
+                def _():
+                    emit(p, i, False)
+
+                return 0
+
+            lax.fori_loop(0, 9, lambda r, c: one(1 + r // 3, 1 + r % 3), 0)
+            lax.fori_loop(1, 4, lambda r, c: one(r, 0), 0)
+            lax.fori_loop(0, 4, lambda r, c: one(0, r), 0)
+
+        def first_shards(p):
+            @pl.when(g > 0)
+            def _():
+                for h in range(2):
+                    send_ov(p, h).wait_recv()
+
+            for i in range(2):
+                emit(p, i, True)
+
+        def summed(p):
+            for o in (1, 3, 2, 0):
+                for h in range(2):
+                    for oa in (1, 3, 2):
+                        send_r(p, h, oa, o).wait_recv()
+                    sbuf[p, h, o] = sbuf[p, h, o] + (
+                        ybuf[p, h, 0, o].astype(F32) + ybuf[p, h, 1, o].astype(F32) + ybuf[p, h, 2, o].astype(F32)
+                    )
+                    if o:
+                        send_v(p, h, o).start()
+
+        along_b(0)
+        own_along_a(0)
+        along_b(1)
 
         q = jnp.concatenate([bdot(lbasis[c], vb[:, 256 * c : 256 * c + 256], NT) for c in range(CL)], axis=0)
         coeffs = dot(ltcat[...], q)
@@ -315,136 +476,24 @@
         ph, pe = split(parents)
         mbuf[pl.ds(pl.multiple_of((32 + d) * K, K), K), :] = jnp.concatenate([qh, ql, ph, pe], axis=1)
 
-        for c in range(4):
-            for h in range(2):
-                b = ab[h][1]
-
-                @pl.when(b != c)
-                def _():
-                    send_p(h, step(b, 4 - c)).wait_recv()
-                    for oa in (1, 3, 2):
-                        send_q(h, oa, step(c + 4 - b, 0)).start()
-
-        for h in range(2):
-            for s in range(2):
-                sa, sb = first(h, s)
-                a, b = ab[h]
-
-                @pl.when(a != sa)
-                def _():
-                    send_q(h, step(a, 4 - sa), step(sb + 4 - b, 0)).wait_recv()
-
-                @pl.when(g > 0)
-                def _():
-                    send_z(h, s).start()
-
-        for h in range(2):
-            a, b = ab[h]
-            for oa in (1, 3, 2):
-                for j in range(4):
-                    from_a, from_b = step(a, 4 - oa), step(b, j)
-                    if h == 0:
-                        early = (from_a == 0) & (from_b < 2)
-                    else:
-                        early = (from_b == 0) & (from_a < 2)
-
-                    @pl.when(jnp.logical_not(early))
-                    def _():
-                        send_q(h, oa, j).wait_recv()
-
-        @pl.when(g < NG - 1)
-        def _():
-            for h in range(2):
-                for s in range(2):
-                    send_z(h, s).wait_recv()
-
+        along_a(0)
+        pass_on(0)
+        own_along_a(1)
+        along_a(1)
+        gathered(0)
         if first_call:
             loads[1].wait()
-
+        loop(near_first)
+        pass_on(1)
+        gathered(1)
         lax.fori_loop(1, ND, lambda o, c: (far_send(o).start(), c)[1], 0)
-
-        n_live = live[0]
-
-        def near(i, carry):
-            for j in range(UNROLL):
-                k = i * UNROLL + j
-                r, c = rows[k], cols[k]
-                weight = jnp.where(k < n_live, table[scl[k]], 0.0)
-                block = blocks[k]
-                vc = jnp.concatenate([w0[c], w1[permuted(c)]], axis=1)
-                vr = jnp.concatenate([w0[r], w1[permuted(r)]], axis=1)
-                to_row = bdot(block, vc, NT).T
-                to_col = bdot(vr, block)
-                seg[2 * k] = seg[prev[2 * k]] + weight * to_row
-                seg[2 * k + 1] = seg[prev[2 * k + 1]] + weight * to_col
-            return carry
-
-        lax.fori_loop(0, NB // UNROLL, near, 0)
-
-        for h in range(2):
-            for o in range(1, 4):
-                send_p(h, o).wait_send()
-                for j in range(4):
-                    send_q(h, o, j).wait_send()
-
-        @pl.when(g > 0)
-        def _():
-            for h in range(2):
-                for s in range(2):
-                    send_z(h, s).wait_send()
-
-        for c in range(NCL, WIN):
-            v = seg[last[c]]
-            t0[c] = v[:, :HALF].astype(BF16)
-            t1[c] = v[:, HALF:].astype(BF16)
-
-        @pl.when(g < NG - 1)
-        def _():
-            for h in range(2):
-                send_ov(h).start()
-
-        def emit(i, extra):
-            place = ((i // 4, i % 4), (i % 4, i // 4))
-            vals = [seg[last[i * CL + c]] for c in range(CL)]
-            for h in range(2):
-                a, b = ab[h]
-                oa, j = step(place[h][0] + 4 - a, 0), step(place[h][1] + 4 - b, 0)
-                at = (place[h][0] * 4 + place[h][1]) * CL
-                parts = [v[:, h * HALF : h * HALF + HALF] for v in vals]
-                if extra:
-                    parts = [p + over[h, i * CL + c].astype(F32) for c, p in enumerate(parts)]
-
-                @pl.when(oa == 0)
-                def _():
-                    for c in range(CL):
-                        sbuf[h, j, c] = parts[c]
-
-                @pl.when(oa != 0)
-                def _():
-                    for c in range(CL):
-                        t[h][at + c] = parts[c].astype(BF16)
-                    send_r(h, oa, j).start()
-
-        def totals(dx, dy):
-            i = step(x, dx) * 4 + step(y, dy)
-
-            @pl.when(i >= 2)
-            def _():
-                emit(i, False)
-
-            return 0
-
-        lax.fori_loop(0, 9, lambda r, c: totals(1 + r // 3, 1 + r % 3), 0)
-        lax.fori_loop(1, 4, lambda r, c: totals(r, 0), 0)
-        lax.fori_loop(0, 4, lambda r, c: totals(0, r), 0)
-
-        @pl.when(g > 0)
-        def _():
-            for h in range(2):
-                send_ov(h).wait_recv()
-
-        for i in range(2):
-            emit(i, True)
+        loop(near_second)
+        overflow(0)
+        totals(0)
+        loop(lambda k, weight: near_row(1, k, weight))
+        overflow(1)
+        totals(1)
+        first_shards(0)
 
         lax.fori_loop(1, ND, lambda o, c: (far_send(o).wait_recv(), c)[1], 0)
         group_rows = pl.ds(32 * K, ND * K)
@@ -468,15 +517,10 @@
         )
         lax.fori_loop(1, NG, lambda o, c: (top_send(o).start(), c)[1], 0)
 
-        for o in (1, 3, 2, 0):
-            for h in range(2):
-                for oa in (1, 3, 2):
-                    send_r(h, oa, o).wait_recv()
-                sbuf[h, o] = sbuf[h, o] + (
-                    ybuf[h, 0, o].astype(F32) + ybuf[h, 1, o].astype(F32) + ybuf[h, 2, o].astype(F32)
-                )
-                if o:
-                    send_v(h, o).start()
+        first_shards(1)
+        summed(0)
+        summed(1)
+
         lax.fori_loop(1, NG, lambda o, c: (top_send(o).wait_recv(), c)[1], 0)
 
         @pl.when(g > 0)
@@ -515,23 +559,32 @@
         def _():
             down.wait_send()
 
-        for h in range(2):
-            for o in (1, 3, 2):
-                send_v(h, o).wait_recv()
-            for c in range(CL):
-                total = sbuf[h, 0, c] + vbuf[h, 0, c] + vbuf[h, 1, c] + vbuf[h, 2, c]
-                lo = 256 * c + h * HALF
-                u[:, lo : lo + HALF] = u[:, lo : lo + HALF] + total
-        for h in range(2):
-            for o in range(1, 4):
-                send_v(h, o).wait_send()
-                for j in range(4):
-                    send_r(h, o, j).wait_send()
-
-        @pl.when(g < NG - 1)
-        def _():
+        for p in range(2):
             for h in range(2):
-                send_ov(h).wait_send()
+                for o in (1, 3, 2):
+                    send_v(p, h, o).wait_recv()
+                for c in range(CL):
+                    total = sbuf[p, h, 0, c] + vbuf[p, h, 0, c] + vbuf[p, h, 1, c] + vbuf[p, h, 2, c]
+                    at = (slice(h * RB, h * RB + RB), slice(256 * c + p * HALF, 256 * c + p * HALF + HALF))
+                    u[at] = u[at] + total
+
+        for p in range(2):
+            for h in range(2):
+                for o in range(1, 4):
+                    send_p(p, h, o).wait_send()
+                    send_v(p, h, o).wait_send()
+                    for j in range(4):
+                        send_q(p, h, o, j).wait_send()
+                        send_r(p, h, o, j).wait_send()
+
+                @pl.when(g > 0)
+                def _():
+                    for s in range(2):
+                        send_z(p, h, s).wait_send()
+
+                @pl.when(g < NG - 1)
+                def _():
+                    send_ov(p, h).wait_send()
 
     row = lax.broadcasted_iota(jnp.int32, (R, R), 0)
     col = lax.broadcasted_iota(jnp.int32, (R, R), 1)
@@ -567,13 +620,13 @@
 
 
 def chains(near_rows, near_cols):
-    target = jnp.stack([near_rows, near_cols], axis=1).reshape(-1)
-    order = jnp.arange(2 * NB, dtype=jnp.int32)
-    before = (target[:, None] == target[None, :]) & (order[None, :] < order[:, None])
-    prev = jnp.max(jnp.where(before, order[None, :], -1), axis=1)
-    hit = jnp.arange(WIN, dtype=jnp.int32)[:, None] == target[None, :]
-    last = jnp.max(jnp.where(hit, order[None, :], -1), axis=1)
-    return jnp.where(prev < 0, 2 * NB, prev), jnp.where(last < 0, 2 * NB, last)
+    target = jnp.stack([near_rows, near_cols])
+    order = jnp.arange(NB, dtype=jnp.int32)
+    before = (target[:, :, None] == target[:, None, :]) & (order[None, :] < order[:, None])[None]
+    prev = jnp.max(jnp.where(before, order, -1), axis=2)
+    hit = jnp.arange(WIN, dtype=jnp.int32)[None, :, None] == target[:, None, :]
+    last = jnp.max(jnp.where(hit, order, -1), axis=2)
+    return jnp.where(prev < 0, NB, prev), jnp.where(last < 0, NB, last)
 
 
 def shards(
@@ -592,15 +645,21 @@
         out_specs=(vmem, vmem),
         scratch_shapes=[
             pltpu.VMEM((NB, 256, 256), BF16),
-            pltpu.VMEM((2 * NB + 1, R, 256), F32),
-            pltpu.VMEM((WIN, R, HALF), BF16),
-            pltpu.VMEM((WIN, R, HALF), BF16),
-            pltpu.VMEM((WIN, R, HALF), BF16),
-            pltpu.VMEM((WIN, R, HALF), BF16),
-            pltpu.VMEM((2, 16, R, HALF), BF16),
-            pltpu.VMEM((2, 3, 4, CL, R, HALF), BF16),
-            pltpu.VMEM((2, 4, CL, R, HALF), F32),
-            pltpu.VMEM((2, 3, CL, R, HALF), F32),
+            pltpu.VMEM((NB + 1, R, 256), F32),
+            pltpu.VMEM((NB + 1, R, HALF), F32),
+            pltpu.VMEM((NB + 1, R, HALF), F32),
+            pltpu.VMEM((WIN, RB, HALF), BF16),
+            pltpu.VMEM((WIN, RB, HALF), BF16),
+            pltpu.VMEM((WIN, RB, HALF), BF16),
+            pltpu.VMEM((WIN, RB, HALF), BF16),
+            pltpu.VMEM((WIN, RB, HALF), BF16),
+            pltpu.VMEM((WIN, RB, HALF), BF16),
+            pltpu.VMEM((WIN, RB, HALF), BF16),
+            pltpu.VMEM((WIN, RB, HALF), BF16),
+            pltpu.VMEM((2, 2, 16, RB, HALF), BF16),
+            pltpu.VMEM((2, 2, 3, 4, CL, RB, HALF), BF16),
+            pltpu.VMEM((2, 2, 4, CL, RB, HALF), F32),
+            pltpu.VMEM((2, 2, 3, CL, RB, HALF), F32),
             pltpu.VMEM((80 * K, 128), BF16),
             pltpu.VMEM((24 * K, 128), BF16),
             pltpu.VMEM((3, ND, 24, 128), F32),

time: 153 us -> 153 us (level)
  no operation moved by 1% of the time
where the time goes in v3:
time: 153 us
  Pallas kernels  146 us (95%)
  local copies, waits for them, and re-layouts  3.2 us (2%)
  other arithmetic  2.29 us (1%)
    pallas_call x1, Pallas kernels, shards(): pl.pallas_call(kernel, out_shape=outs, in_specs=[smem] * 7 + [anywhere] *...  146 us
    unnamed x2, local copies, waits for them, and re-layouts  3.2 us

profile of v3, /device:TPU:1, one launch (start us, length us, event | category | flops | bytes accessed | tf_op | source)
XLA Modules:
  0.0 153.2 jit_solution(16026526307121803844)
XLA Ops:
  1.3 0.7 pad_add_fusion
  2.0 0.2 select_reduce_fusion.1
  2.1 0.6 compare_select_fusion.last
  2.7 0.2 select_reduce_fusion
  3.0 0.6 compare_select_fusion.1.prev
  3.6 146.4 %arnoldi.1 = (f32[32,2048]{1,0:T(8,128)}, f32[5,32,32]{2,1,0:T(8,128)}) custom-call(s32[160]{0:T(256)} %rows.1, s32[160]{0:T(256)} %cols.1, s32[160]{0:T(256)} %scl.1, f32[256]{0:T(256)} %table.1, s32[1]{0:T(128)S(6)} %copy.16.live, s32[2,160]{1,0:T(2,128)} %compare_select_fusion.1.prev, s32[2,144]{1,0:T(2,128)} %compare_select_fusion.last, ...), custom_call_target="tpu_custom_call" | custom-call | tf_op jit(solution)/shard_map/arnoldi/pallas_call | solution.py:641
  150.0 1.7 %copy.17 = f32[32,2048]{1,0:T(8,128)} copy(f32[32,2048]{1,0:T(8,128)} %get-tuple-element.4) | data formatting | bytes 524288
  151.7 1.5 copy.18
  (1 shorter events, 0.0 us)

commit v4 on v3

--- a/solution.py
+++ b/solution.py
@@ -468,6 +468,7 @@
         along_b(0)
         own_along_a(0)
         along_b(1)
+        own_along_a(1)
 
         q = jnp.concatenate([bdot(lbasis[c], vb[:, 256 * c : 256 * c + 256], NT) for c in range(CL)], axis=0)
         coeffs = dot(ltcat[...], q)
@@ -478,7 +479,6 @@
 
         along_a(0)
         pass_on(0)
-        own_along_a(1)
         along_a(1)
         gathered(0)
         if first_call:

time: 153 us -> 154 us (level)
  no operation moved by 1% of the time
where the time goes in v4:
time: 154 us
  Pallas kernels  147 us (95%)
  local copies, waits for them, and re-layouts  3.2 us (2%)
  other arithmetic  2.29 us (1%)
    pallas_call x1, Pallas kernels, shards(): pl.pallas_call(kernel, out_shape=outs, in_specs=[smem] * 7 + [anywhere] *...  147 us
    unnamed x2, local copies, waits for them, and re-layouts  3.2 us

profile of v4, /device:TPU:1, one launch (start us, length us, event | category | flops | bytes accessed | tf_op | source)
XLA Modules:
  0.0 153.8 jit_solution(9135336959942314352)
XLA Ops:
  1.3 0.7 pad_add_fusion
  2.0 0.2 select_reduce_fusion.1
  2.1 0.6 compare_select_fusion.last
  2.7 0.2 select_reduce_fusion
  3.0 0.6 compare_select_fusion.1.prev
  3.6 147.1 %arnoldi.1 = (f32[32,2048]{1,0:T(8,128)}, f32[5,32,32]{2,1,0:T(8,128)}) custom-call(s32[160]{0:T(256)} %rows.1, s32[160]{0:T(256)} %cols.1, s32[160]{0:T(256)} %scl.1, f32[256]{0:T(256)} %table.1, s32[1]{0:T(128)S(6)} %copy.16.live, s32[2,160]{1,0:T(2,128)} %compare_select_fusion.1.prev, s32[2,144]{1,0:T(2,128)} %compare_select_fusion.last, ...), custom_call_target="tpu_custom_call" | custom-call | tf_op jit(solution)/shard_map/arnoldi/pallas_call | solution.py:641
  150.6 1.7 %copy.17 = f32[32,2048]{1,0:T(8,128)} copy(f32[32,2048]{1,0:T(8,128)} %get-tuple-element.4) | data formatting | bytes 524288
  152.3 1.5 copy.18
  (1 shorter events, 0.0 us)
